TPU v7x, 512 devices: a whole 4x4x16 slice. The times are simulated.
512 devices in a mesh: filt: 32 (over z_lo, x, core), dp: 16 (over z_hi, y).
Axes of the slice: x: 4, y: 4, z: 16 (z_hi: 4, z_lo: 4; z = z_hi * 4 + z_lo), core: 2. Of those that a mesh axis runs over, the one named last changes fastest.
Arguments:
- activations: bfloat16 [16, 128, 4, 32, 128], P('dp', 'filt'), may hold values from -6 to 6
- weight_one: bfloat16 [3, 3, 3, 128, 128], P(None, None, None, None, 'filt'), may hold values from -0.109375 to 0.109375
- weight_two: bfloat16 [3, 3, 3, 128, 128], P(None, None, None, None, 'filt'), may hold values from -0.109375 to 0.109375
- grad_out: bfloat16 [16, 128, 4, 32, 128], P('dp', 'filt'), may hold values from -0.011962891 to 0.011962891
Outputs:
- out_two: bfloat16 [16, 128, 4, 32, 128], P('dp', 'filt')
- grad_one: float32 [3, 3, 3, 128, 128], P(None, None, None, None, 'filt')
- grad_two: float32 [3, 3, 3, 128, 128], P(None, None, None, None, 'filt')
All inputs are finite; a program needn't handle non-finite values.
Results may differ from a plain program's by a relative error of at most 0.035.
The roundings to bfloat16 on the way count: a program that leaves them out, or rounds other values in their place, can miss the bound.
Values may be sent and summed in bfloat16 or wider, within the bound.
No kernel may reach another device: no remote copies, remote signals or barrier semaphores. Data moves between devices by JAX's collectives and lax.ppermute only.
A program may use at most 64 MiB of HBM per device.

v0:
```python
import jax
import jax.numpy as jnp
from jax import lax
from jax.sharding import PartitionSpec as P

SLOPE = 0.3


def with_halo(array, sides, width):
    for axis, dim in sides:
        peers, length = (lax.axis_size(axis), array.shape[dim])
        up = [(i, (i + 1) % peers) for i in range(peers - 1)]
        down = [(j, i) for i, j in up]
        last = lax.slice_in_dim(array, length - width, length, axis=dim)
        leading = lax.slice_in_dim(array, 0, width, axis=dim)
        before = lax.ppermute(last, axis, up)
        after = lax.ppermute(leading, axis, down)
        array = jnp.concatenate([before, array, after], axis=dim)
    return array


def leaky_relu(values):
    return jnp.where(values > 0, values, SLOPE * values)


def slope_of(values):
    return jnp.where(values > 0, jnp.float32(1.0), jnp.float32(SLOPE))


def convolve_rows(padded, weight):
    return lax.conv_general_dilated(
        padded,
        weight,
        (1, 1, 1),
        [(1, 1), (0, 0), (1, 1)],
        dimension_numbers=("NCDHW", "DHWIO", "NCDHW"),
        preferred_element_type=jnp.float32,
    )


def tap_grad(padded, errors):
    depth = errors.shape[2]
    rows = errors.shape[3]
    width = errors.shape[4]
    framed = jnp.pad(padded, ((0, 0), (0, 0), (1, 1), (0, 0), (1, 1)))
    flat_errors = errors[0].reshape(errors.shape[1], -1)
    layers = []
    for depth_at in range(3):
        windows = [
            framed[
                0, :, depth_at : depth_at + depth, row_at : row_at + rows, col_at : col_at + width
            ].reshape(framed.shape[1], -1)
            for row_at in range(3)
            for col_at in range(3)
        ]
        stacked = jnp.stack(windows, 0)
        layers.append(
            jnp.einsum("kiv,ov->kio", stacked, flat_errors, preferred_element_type=jnp.float32)
        )
    return jnp.concatenate(layers, 0).reshape(3, 3, 3, framed.shape[1], errors.shape[1])


def reduce_grad(partial_grad):
    summed = lax.psum(partial_grad.astype(jnp.bfloat16), "dp")
    return lax.psum_scatter(summed, "filt", scatter_dimension=4, tiled=True).astype(jnp.float32)


def on_device(activations, weight_one, weight_two, grad_out):
    volume, cotangent = (
        lax.all_to_all(activations, "filt", split_axis=3, concat_axis=1, tiled=True),
        lax.all_to_all(grad_out, "filt", split_axis=3, concat_axis=1, tiled=True),
    )
    full_one = lax.all_gather(weight_one, "filt", axis=4, tiled=True)
    full_two = lax.all_gather(weight_two, "filt", axis=4, tiled=True)
    volume_rim = with_halo(volume, (("filt", 3),), 1)
    pre_one = convolve_rows(volume_rim, full_one)
    hidden = leaky_relu(pre_one).astype(jnp.bfloat16)
    hidden_rim = with_halo(hidden, (("filt", 3),), 1)
    pre_two = convolve_rows(hidden_rim, full_two)
    output = leaky_relu(pre_two).astype(jnp.bfloat16)
    result = lax.all_to_all(output, "filt", split_axis=1, concat_axis=3, tiled=True)
    error_two = (cotangent.astype(jnp.float32) * slope_of(pre_two)).astype(jnp.bfloat16)
    grad_two = reduce_grad(tap_grad(hidden_rim, error_two))
    error_rim = with_halo(error_two, (("filt", 3),), 1)
    flipped = jnp.transpose(full_two[::-1, ::-1, ::-1], (0, 1, 2, 4, 3))
    back_one = convolve_rows(error_rim, flipped)
    error_one = (back_one * slope_of(pre_one)).astype(jnp.bfloat16)
    grad_one = reduce_grad(tap_grad(volume_rim, error_one))
    return (result, grad_one, grad_two)


def solution(mesh):
    placed = (
        P("dp", "filt", None, None, None),
        P(None, None, None, None, "filt"),
        P(None, None, None, None, "filt"),
        P("dp", "filt", None, None, None),
    )
    return jax.shard_map(
        on_device,
        mesh=mesh,
        in_specs=placed,
        out_specs=(
            P("dp", "filt", None, None, None),
            P(None, None, None, None, "filt"),
            P(None, None, None, None, "filt"),
        ),
        check_vma=False,
    )
```

profile of v0, /device:TPU:2, one launch (start us, length us, event | category | flops | bytes accessed | tf_op | source)
XLA Modules:
  0.0 684.0 jit_solution(7017394732347407726)
XLA Ops:
  7.2 1.6 copy.247
  8.8 9.4 %all-to-all-start = ((bf16[1,4,4,32,128]{4,2,1,0,3:T(4,128)(2,1)}), bf16[1,4,4,32,128]{4,2,1,0,3:T(4,128)(2,1)S(1)}, u32[]{:S(2)}, u32[]{:S(2)}) async-start(bf16[1,4,4,32,128]{4,2,1,0,3:T(4,128)(2,1)} %copy.247), calls=%async_computation | async-start | bytes 262144 | tf_op jit(solution)/shard_map/all_to_all | solution.py:70
  19.0 1.6 copy.271
  20.6 5.2 all-to-all-done
  25.8 5.0 all-to-all-start.2
  30.9 42.3 %all_gather.6 = bf16[3,3,3,128,128]{3,2,1,0,4:T(4,128)(2,1)S(1)} all-gather(bf16[3,3,3,128,4]{3,2,1,0,4:T(4,128)(2,1)S(1)} %copy.252), channel_id=1, replica_groups=mesh['filt'=32,'dp'=16] {'filt'}, dimensions={4}, use_global_device_ids=true | all-gather | bytes 912384 | tf_op jit(solution)/shard_map/all_gather | solution.py:73
  73.2 48.0 %all_gather.7 = bf16[3,3,3,128,128]{3,2,1,0,4:T(4,128)(2,1)} all-gather(bf16[3,3,3,128,4]{3,2,1,0,4:T(4,128)(2,1)S(1)} %copy.257), channel_id=1, replica_groups=mesh['filt'=32,'dp'=16] {'filt'}, dimensions={4}, use_global_device_ids=true | all-gather | bytes 912384 | tf_op jit(solution)/shard_map/all_gather | solution.py:74
  121.2 2.3 collective-permute-start
  123.5 3.3 collective-permute-start.1
  130.6 1.9 fusion.26
  132.6 2.4 collective-permute-start.2
  135.0 3.5 collective-permute-start.3
  151.0 1.6 stack_reshape_squeeze.172
  152.7 1.7 copy.283
  156.0 1.7 copy.284
  157.7 1.6 stack_reshape_squeeze.174
  159.3 1.7 copy.285
  162.5 1.7 copy.286
  164.2 1.6 stack_reshape_squeeze.177
  177.3 1.7 copy.295
  179.0 1.6 stack_reshape_squeeze.186
  180.6 1.7 copy.296
  182.3 1.6 stack_reshape_squeeze.187
  192.6 2.3 pad_slice_fusion.39
  197.2 1.8 compare_select_fusion
  201.7 1.9 collective-permute-start.4
  203.6 3.9 collective-permute-start.5
  215.4 1.7 stack_reshape_squeeze.192
  217.9 1.7 stack_reshape_squeeze.193
  222.1 1.6 stack_reshape_squeeze.195
  226.9 1.6 stack_reshape_squeeze.197
  235.8 1.6 stack_reshape_squeeze.200
  240.0 1.6 stack_reshape_squeeze.204
  242.4 1.7 stack_reshape_squeeze.205
  244.9 1.7 stack_reshape_squeeze.206
  251.9 1.8 convolution_convert_fusion.2
  259.2 1.7 copy.325
  261.9 1.7 copy.326
  265.3 1.7 copy.327
  268.6 1.7 copy.328
  277.2 1.7 convolution_convert_fusion
  279.1 1.7 copy.330
  285.8 1.7 convolution_convert_fusion.3
  287.6 1.7 copy.298
  291.1 4.1 all-to-all-start.1
  297.1 5.6 all-to-all-done.1
  303.4 272.9 %all-reduce.8.cloned.1.call-done = (bf16[3,3,3,128,128]{3,4,2,1,0:T(8,128)(2,1)}, bf16[3,3,3,128,128]{3,4,2,1,0:T(8,128)(2,1)}) async-done(((bf16[3,3,3,128,128]{3,4,2,1,0:T(8,128)(2,1)}, bf16[3,3,3,128,128]{3,4,2,1,0:T(8,128)(2,1)}), (bf16[3,3,3,128,128]{3,4,2,1,0:T(8,128)(2,1)}, bf16[3,3,3,128,128]{3,4,2,1,0:T(8,128)(2,1)})) %all-reduce.8.cloned.1.call-update) | async-done | bytes 1769488
  577.1 98.8 %all-reduce.5 = (bf16[3,3,3,128,4]{3,4,2,1,0:T(4,128)(2,1)S(1)}, bf16[3,3,3,128,4]{3,4,2,1,0:T(4,128)(2,1)S(1)}) all-reduce(bf16[3,3,3,128,4]{3,4,2,1,0:T(4,128)(2,1)S(1)} %get-tuple-element.74, bf16[3,3,3,128,4]{3,4,2,1,0:T(4,128)(2,1)S(1)} %get-tuple-element.73), channel_id=1, replica_groups=mesh['filt'=32,'dp'=16] {'dp'}, use_global_device_ids=true, to_apply=%region_0.1 | all-reduce | flops 27648 | bytes 110592 | tf_op jit(solution)/shard_map/psum | solution.py:64
  (340 shorter events, 104.0 us)
Async XLA Ops:
  7.2 66.0 %copy-start.69 = (bf16[3,3,3,128,4]{3,4,2,1,0:T(4,128)(2,1)S(1)}, bf16[3,3,3,128,4]{3,4,2,1,0:T(4,128)(2,1)}, u32[]{:S(2)}) copy-start(bf16[3,3,3,128,4]{3,4,2,1,0:T(4,128)(2,1)} %param.6) | copy-start | bytes 82948
  8.8 17.0 %all-to-all-start = ((bf16[1,4,4,32,128]{4,2,1,0,3:T(4,128)(2,1)}), bf16[1,4,4,32,128]{4,2,1,0,3:T(4,128)(2,1)S(1)}, u32[]{:S(2)}, u32[]{:S(2)}) async-start(bf16[1,4,4,32,128]{4,2,1,0,3:T(4,128)(2,1)} %copy.247), calls=%async_computation | async-start | bytes 262144 | tf_op jit(solution)/shard_map/all_to_all | solution.py:70
  25.8 101.7 %all-to-all-start.2 = ((bf16[1,4,4,32,128]{4,2,1,0,3:T(4,128)(2,1)}), bf16[1,4,4,32,128]{4,2,1,0,3:T(4,128)(2,1)S(1)}, u32[]{:S(2)}, u32[]{:S(2)}) async-start(bf16[1,4,4,32,128]{4,2,1,0,3:T(4,128)(2,1)} %copy.271), calls=%async_computation.2 | async-start | bytes 262144 | tf_op jit(solution)/shard_map/all_to_all | solution.py:71
  30.8 545.4 %all-reduce.8.cloned.1.call-start = ((), (), s32[]{:S(2)}) async-start(), calls=%async_computation.3 | async-start | bytes 3538944
  121.2 7.1 %collective-permute-start = (bf16[1,128,4,1,128]{4,1,2,3,0:T(8,128)(2,1)S(1)}, bf16[1,128,4,1,128]{4,1,2,3,0:T(8,128)(2,1)S(1)}, u32[]{:S(2)}, u32[]{:S(2)}) collective-permute-start(bf16[1,128,4,1,128]{4,1,2,3,0:T(8,128)(2,1)S(1)} %bitcast.200), channel_id=1, source_target_pairs={{0,16},{16,32},{32,48},{48,64},{64,80},{80,96},{96,112},{112,128},... | collective-permute-start | bytes 393224 | tf_op jit(solution)/shard_map/ppermute | solution.py:16
  123.5 5.8 collective-permute-start.1
  132.6 59.7 %collective-permute-start.2 = (bf16[1,128,4,1,128]{1,2,4,0,3:T(4,128)(2,1)S(1)}, bf16[1,128,4,1,128]{1,2,4,0,3:T(4,128)(2,1)S(1)}, u32[]{:S(2)}, u32[]{:S(2)}) collective-permute-start(bf16[1,128,4,1,128]{1,2,4,0,3:T(4,128)(2,1)S(1)} %slice_bitcast_fusion.2), channel_id=1, source_target_pairs={{0,16},{16,32},{32,48},{48,64},{64,80},{80,96},{96,112},{112,128},... | collective-permute-start | bytes 393224 | tf_op jit(solution)/shard_map/ppermute | solution.py:16
  135.0 57.3 %collective-permute-start.3 = (bf16[1,128,4,1,128]{1,2,4,0,3:T(4,128)(2,1)S(1)}, bf16[1,128,4,1,128]{1,2,4,0,3:T(4,128)(2,1)S(1)}, u32[]{:S(2)}, u32[]{:S(2)}) collective-permute-start(bf16[1,128,4,1,128]{1,2,4,0,3:T(4,128)(2,1)S(1)} %slice_bitcast_fusion.2), channel_id=1, source_target_pairs={{16,0},{32,16},{48,32},{64,48},{80,64},{96,80},{112,96},{128,112},... | collective-permute-start | bytes 393224 | tf_op jit(solution)/shard_map/ppermute | solution.py:17
  146.1 4.2 copy-start.13
  151.0 14.8 %copy-start.11 = (bf16[1,128,4,1,128]{4,1,2,3,0:T(8,128)(2,1)S(1)}, bf16[1,128,4,1,128]{4,1,2,3,0:T(8,128)(2,1)}, u32[]{:S(2)}) copy-start(bf16[1,128,4,1,128]{4,1,2,3,0:T(8,128)(2,1)} %copy-done.10) | copy-start | bytes 393220
  175.0 8.9 %copy-start.29 = (bf16[1,128,512]{2,1,0:T(8,128)(2,1)S(1)}, bf16[1,128,512]{2,1,0:T(8,128)(2,1)}, u32[]{:S(2)}) copy-start(bf16[1,128,512]{2,1,0:T(8,128)(2,1)} %stack_reshape_squeeze.163) | copy-start | bytes 393220
  175.7 8.3 %copy-start.30 = (bf16[1,128,512]{2,1,0:T(8,128)(2,1)S(1)}, bf16[1,128,512]{2,1,0:T(8,128)(2,1)}, u32[]{:S(2)}) copy-start(bf16[1,128,512]{2,1,0:T(8,128)(2,1)} %stack_reshape_squeeze.164) | copy-start | bytes 393220
  175.8 8.2 %copy-start.31 = (bf16[1,128,512]{2,1,0:T(8,128)(2,1)S(1)}, bf16[1,128,512]{2,1,0:T(8,128)(2,1)}, u32[]{:S(2)}) copy-start(bf16[1,128,512]{2,1,0:T(8,128)(2,1)} %stack_reshape_squeeze.165) | copy-start | bytes 393220
  176.5 7.5 %copy-start.32 = (bf16[1,128,512]{2,1,0:T(8,128)(2,1)S(1)}, bf16[1,128,512]{2,1,0:T(8,128)(2,1)}, u32[]{:S(2)}) copy-start(bf16[1,128,512]{2,1,0:T(8,128)(2,1)} %stack_reshape_squeeze.166) | copy-start | bytes 393220
  176.6 7.5 %copy-start.33 = (bf16[1,128,512]{2,1,0:T(8,128)(2,1)S(1)}, bf16[1,128,512]{2,1,0:T(8,128)(2,1)}, u32[]{:S(2)}) copy-start(bf16[1,128,512]{2,1,0:T(8,128)(2,1)} %stack_reshape_squeeze.167) | copy-start | bytes 393220
  177.3 6.8 copy-start.34
  185.2 4.0 copy-start.50
  185.2 4.7 copy-start.51
  185.9 5.6 copy-start.67
  199.3 13.6 %copy-start.26 = (bf16[1,128,4,1,128]{1,2,4,0,3:T(4,128)(2,1)S(1)}, bf16[1,128,4,1,128]{1,2,4,0,3:T(4,128)(2,1)}, u32[]{:S(2)}) copy-start(bf16[1,128,4,1,128]{1,2,4,0,3:T(4,128)(2,1)} %get-tuple-element.21) | copy-start | bytes 393220
  200.6 14.0 %copy-start.25 = (bf16[1,128,4,1,128]{1,2,4,0,3:T(4,128)(2,1)S(1)}, bf16[1,128,4,1,128]{1,2,4,0,3:T(4,128)(2,1)}, u32[]{:S(2)}) copy-start(bf16[1,128,4,1,128]{1,2,4,0,3:T(4,128)(2,1)} %get-tuple-element.22) | copy-start | bytes 393220
  201.7 79.0 %collective-permute-start.4 = (bf16[1,128,4,1,128]{4,1,2,3,0:T(8,128)(2,1)}, bf16[1,128,4,1,128]{4,1,2,3,0:T(8,128)(2,1)}, u32[]{:S(2)}, u32[]{:S(2)}) collective-permute-start(bf16[1,128,4,1,128]{4,1,2,3,0:T(8,128)(2,1)} %fusion.28), channel_id=1, source_target_pairs={{0,16},{16,32},{32,48},{48,64},{64,80},{80,96},{96,112},{112,128},... | collective-permute-start | bytes 393224 | tf_op jit(solution)/shard_map/ppermute | solution.py:16
  203.6 77.1 %collective-permute-start.5 = (bf16[1,128,4,1,128]{4,1,2,3,0:T(8,128)(2,1)}, bf16[1,128,4,1,128]{4,1,2,3,0:T(8,128)(2,1)}, u32[]{:S(2)}, u32[]{:S(2)}) collective-permute-start(bf16[1,128,4,1,128]{4,1,2,3,0:T(8,128)(2,1)} %fusion.28), channel_id=1, source_target_pairs={{16,0},{32,16},{48,32},{64,48},{80,64},{96,80},{112,96},{128,112},... | collective-permute-start | bytes 393224 | tf_op jit(solution)/shard_map/ppermute | solution.py:17
  207.5 9.6 %copy-start.24 = (bf16[1,128,4,1,128]{1,2,4,0,3:T(4,128)(2,1)S(1)}, bf16[1,128,4,1,128]{1,2,4,0,3:T(4,128)(2,1)}, u32[]{:S(2)}) copy-start(bf16[1,128,4,1,128]{1,2,4,0,3:T(4,128)(2,1)} %get-tuple-element.23) | copy-start | bytes 393220
  209.4 10.2 %copy-start.23 = (bf16[1,128,4,1,128]{1,2,4,0,3:T(4,128)(2,1)S(1)}, bf16[1,128,4,1,128]{1,2,4,0,3:T(4,128)(2,1)}, u32[]{:S(2)}) copy-start(bf16[1,128,4,1,128]{1,2,4,0,3:T(4,128)(2,1)} %get-tuple-element.24) | copy-start | bytes 393220
  211.2 10.1 %copy-start.22 = (bf16[1,128,4,1,128]{1,2,4,0,3:T(4,128)(2,1)S(1)}, bf16[1,128,4,1,128]{1,2,4,0,3:T(4,128)(2,1)}, u32[]{:S(2)}) copy-start(bf16[1,128,4,1,128]{1,2,4,0,3:T(4,128)(2,1)} %get-tuple-element.25) | copy-start | bytes 393220
  213.6 10.1 %copy-start.21 = (bf16[1,128,4,1,128]{1,2,4,0,3:T(4,128)(2,1)S(1)}, bf16[1,128,4,1,128]{1,2,4,0,3:T(4,128)(2,1)}, u32[]{:S(2)}) copy-start(bf16[1,128,4,1,128]{1,2,4,0,3:T(4,128)(2,1)} %get-tuple-element.26) | copy-start | bytes 393220
  215.4 10.7 %copy-start.20 = (bf16[1,128,4,1,128]{1,2,4,0,3:T(4,128)(2,1)S(1)}, bf16[1,128,4,1,128]{1,2,4,0,3:T(4,128)(2,1)}, u32[]{:S(2)}) copy-start(bf16[1,128,4,1,128]{1,2,4,0,3:T(4,128)(2,1)} %get-tuple-element.19) | copy-start | bytes 393220
  217.9 10.7 %copy-start.19 = (bf16[1,128,4,1,128]{1,2,4,0,3:T(4,128)(2,1)S(1)}, bf16[1,128,4,1,128]{1,2,4,0,3:T(4,128)(2,1)}, u32[]{:S(2)}) copy-start(bf16[1,128,4,1,128]{1,2,4,0,3:T(4,128)(2,1)} %get-tuple-element.27) | copy-start | bytes 393220
  223.7 11.3 %copy-start.18 = (bf16[1,128,4,1,128]{1,2,4,0,3:T(4,128)(2,1)S(1)}, bf16[1,128,4,1,128]{1,2,4,0,3:T(4,128)(2,1)}, u32[]{:S(2)}) copy-start(bf16[1,128,4,1,128]{1,2,4,0,3:T(4,128)(2,1)} %get-tuple-element.28) | copy-start | bytes 393220
  226.1 11.3 %copy-start.17 = (bf16[1,128,4,1,128]{1,2,4,0,3:T(4,128)(2,1)S(1)}, bf16[1,128,4,1,128]{1,2,4,0,3:T(4,128)(2,1)}, u32[]{:S(2)}) copy-start(bf16[1,128,4,1,128]{1,2,4,0,3:T(4,128)(2,1)} %get-tuple-element.29) | copy-start | bytes 393220
  228.6 9.7 %copy-start.16 = (bf16[1,128,4,1,128]{1,2,4,0,3:T(4,128)(2,1)S(1)}, bf16[1,128,4,1,128]{1,2,4,0,3:T(4,128)(2,1)}, u32[]{:S(2)}) copy-start(bf16[1,128,4,1,128]{1,2,4,0,3:T(4,128)(2,1)} %get-tuple-element.30) | copy-start | bytes 393220
  231.0 8.2 %copy-start.15 = (bf16[1,128,4,1,128]{1,2,4,0,3:T(4,128)(2,1)S(1)}, bf16[1,128,4,1,128]{1,2,4,0,3:T(4,128)(2,1)}, u32[]{:S(2)}) copy-start(bf16[1,128,4,1,128]{1,2,4,0,3:T(4,128)(2,1)} %get-tuple-element.31) | copy-start | bytes 393220
  235.8 8.3 %copy-start.14 = (bf16[1,128,4,1,128]{1,2,4,0,3:T(4,128)(2,1)S(1)}, bf16[1,128,4,1,128]{1,2,4,0,3:T(4,128)(2,1)}, u32[]{:S(2)}) copy-start(bf16[1,128,4,1,128]{1,2,4,0,3:T(4,128)(2,1)} %get-tuple-element.32) | copy-start | bytes 393220
  237.6 9.0 %copy-start.49 = (bf16[1,128,512]{2,1,0:T(8,128)(2,1)S(1)}, bf16[1,128,512]{2,1,0:T(8,128)(2,1)}, u32[]{:S(2)}) copy-start(bf16[1,128,512]{2,1,0:T(8,128)(2,1)} %stack_reshape_squeeze.190) | copy-start | bytes 393220
  238.5 9.4 %copy-start.52 = (bf16[1,128,512]{2,1,0:T(8,128)(2,1)S(1)}, bf16[1,128,512]{2,1,0:T(8,128)(2,1)}, u32[]{:S(2)}) copy-start(bf16[1,128,512]{2,1,0:T(8,128)(2,1)} %stack_reshape_squeeze.192) | copy-start | bytes 393220
  239.2 9.4 %copy-start.53 = (bf16[1,128,512]{2,1,0:T(8,128)(2,1)S(1)}, bf16[1,128,512]{2,1,0:T(8,128)(2,1)}, u32[]{:S(2)}) copy-start(bf16[1,128,512]{2,1,0:T(8,128)(2,1)} %stack_reshape_squeeze.193) | copy-start | bytes 393220
  241.6 8.3 %copy-start.54 = (bf16[1,128,512]{2,1,0:T(8,128)(2,1)S(1)}, bf16[1,128,512]{2,1,0:T(8,128)(2,1)}, u32[]{:S(2)}) copy-start(bf16[1,128,512]{2,1,0:T(8,128)(2,1)} %stack_reshape_squeeze.195) | copy-start | bytes 393220
  242.4 8.1 %copy-start.55 = (bf16[1,128,512]{2,1,0:T(8,128)(2,1)S(1)}, bf16[1,128,512]{2,1,0:T(8,128)(2,1)}, u32[]{:S(2)}) copy-start(bf16[1,128,512]{2,1,0:T(8,128)(2,1)} %stack_reshape_squeeze.196) | copy-start | bytes 393220
  244.9 6.3 copy-start.56
  249.9 3.8 copy-start
  249.9 3.8 copy-start.57
  254.7 3.7 copy-start.8
  254.7 3.9 copy-start.7
  271.9 4.0 copy-start.65
  271.9 4.6 copy-start.66
  275.2 3.7 copy-start.3
  291.1 11.6 %all-to-all-start.1 = ((bf16[1,128,4,1,128]{4,2,3,0,1:T(4,128)(2,1)}), bf16[1,128,4,1,128]{4,2,3,0,1:T(4,128)(2,1)S(1)}, u32[]{:S(2)}, u32[]{:S(2)}) async-start(bf16[1,128,4,1,128]{4,2,3,0,1:T(4,128)(2,1)} %copy.260), calls=%async_computation.1 | async-start | bytes 262144 | tf_op jit(solution)/shard_map/all_to_all | solution.py:81
  (34 other events, 54.3 us)
Sparse Core Ops, SparseCore 0:
  289.5 286.7 all-reduce.7
where the time goes:
time: 686 us; the launch traced here: 684 us
  waiting for transfers between devices  285 us (42%)
  blocking collectives  189 us (28%)
  local copies, waits for them, and re-layouts  143 us (21%)
  starting transfers between devices  35.7 us (5%)
  between operations  15.7 us (2%)
  matrix products  12.2 us (2%)
    unnamed x2, waiting for transfers between devices  273 us
    psum x1, blocking collectives, reduce_grad(): summed = lax.psum(partial_grad.astype(jnp.bfloat16), 'dp')  98.8 us
    another operation x60, local copies, waits for them, and re-layouts, tap_grad(): stacked = jnp.stack(windows, 0)  57.6 us
    all_gather x1, blocking collectives, on_device(): full_two = lax.all_gather(weight_two, 'filt', axis=4, tiled=True)  48 us
    all_gather x1, blocking collectives, on_device(): full_one = lax.all_gather(weight_one, 'filt', axis=4, tiled=True)  42.3 us
    slice x52, local copies, waits for them, and re-layouts, tap_grad(): framed[0, :, depth_at:depth_at + depth, row_at:row_at + rows, col_at:col_...  39.9 us
    unnamed x202, local copies, waits for them, and re-layouts  34.6 us
  transfers between devices with their start and end apart: 10, of which 4 were waited for; matrix products, arithmetic and copies ran while one was open for 19% of the time, Pallas kernels for 0%

commit v1 on v0

v1 whole, which is shorter than its diff:
```python
import jax
import jax.numpy as jnp
import numpy as np
from jax import lax
from jax.experimental import pallas as pl
from jax.experimental.pallas import tpu as pltpu
from jax.sharding import Mesh, PartitionSpec as P

SLOPE = 0.3
CHIPS = ("zl", "x")
FILT = ("zl", "x", "c")
DP = ("zh", "y")
F32 = jnp.float32
BF16 = jnp.bfloat16
ROWS, COTS, TAPS = 8, 4, 28


def low_half(shape):
    return lax.broadcasted_iota(jnp.int32, shape, len(shape) - 2) < 4


def swap_halves(tiles):
    return pltpu.roll(tiles, 4, tiles.ndim - 2)


def merge(mine, other, core):
    low = low_half(mine.shape)
    first = jnp.where(low, mine, swap_halves(other))
    second = jnp.where(low, swap_halves(mine), other)
    return [pltpu.roll(plane, 4 * core, plane.ndim - 2) for plane in (first, second)]


def shift_lanes(block, by):
    lane = lax.broadcasted_iota(jnp.int32, block.shape, 1)
    edge = 0 if by > 0 else 127
    return jnp.where(lane == edge, 0.0, pltpu.roll(block, by % 128, 1))


def conv_plane(weights, source, depth, rows, first_row):
    low, high = max(depth - 1, 0), min(depth + 1, 3)
    taps = slice((low - depth + 1) * 128, (high - depth + 2) * 128)
    total = None
    for b in range(3):
        lanes = slice((first_row + b) * 128, (first_row + b + rows) * 128)
        part = jnp.dot(
            weights[b, :, taps],
            source[low * 128 : (high + 1) * 128, lanes],
            preferred_element_type=F32,
        )
        total = part if total is None else total + part
    out = []
    for r in range(rows):
        block = total[:, r * 128 : (r + 1) * 128]
        out.append(
            block[128:256] + shift_lanes(block[:128], 1) + shift_lanes(block[256:], -1)
        )
    return out


def own_rows(block, core):
    tiles = pltpu.roll(block.reshape(4, 4, 8, 128), (8 - 4 * core) % 8, 2)
    pairs = []
    for x in range(4):
        for zl in (0, 2):
            one, two = tiles[zl, x], tiles[zl + 1, x]
            pairs.append(jnp.where(low_half(one.shape), one, swap_halves(two)))
    return jnp.concatenate(pairs, 0)


def put_errors(shifted, block, core, depth, row):
    own = own_rows(block, core)
    lanes = slice((depth * 2 + row) * 128, (depth * 2 + row + 1) * 128)
    shifted[0:64, lanes] = shift_lanes(own, -1).astype(BF16)
    shifted[64:128, lanes] = own.astype(BF16)
    shifted[128:192, lanes] = shift_lanes(own, 1).astype(BF16)


def tap_grad(shifted, source, first_row, total, out, which):
    for b in range(3):
        lanes = slice((first_row + b) * 128, (first_row + b + 2) * 128)
        total[...] = jnp.zeros_like(total)
        for depth in range(4):
            low, high = max(depth - 1, 0), min(depth + 1, 3)
            taps = slice((low - depth + 1) * 128, (high - depth + 2) * 128)
            total[:, taps] += lax.dot_general(
                shifted[:, depth * 256 : (depth + 1) * 256],
                source[low * 128 : (high + 1) * 128, lanes],
                (((1,), (1,)), ((), ())),
                preferred_element_type=F32,
            )
        for a in range(3):
            for e in range(3):
                tap = a * 9 + b * 3 + e
                for x in range(4):
                    out[x, tap // 7, which * 7 + tap % 7] = total[
                        e * 64 + x * 16 : e * 64 + (x + 1) * 16, a * 128 : (a + 1) * 128
                    ].astype(BF16)


def work(
    place, mine, other, out_tiles, grads,
    act, hid, err, cot, w_one, w_two, w_back, pre, shifted, total,
):
    core, chip = place[0], place[1]

    def planes(step, h):
        one = mine[:, step].astype(F32).reshape(16, 2, 8, 128)[:, h]
        two = other[:, step].astype(F32).reshape(16, 2, 8, 128)[:, h]
        return [plane.reshape(128, 128) for plane in merge(one, two, core)]

    for r in range(ROWS):
        for h in range(2):
            for p, plane in enumerate(planes(r, h)):
                z = 2 * h + p
                act[z * 128 : (z + 1) * 128, r * 128 : (r + 1) * 128] = plane.astype(BF16)
    for layer in range(2):
        for step in range(7):
            for h in range(2):
                for p, plane in enumerate(planes(ROWS + COTS + layer * 7 + step, h)):
                    tap = 4 * step + 2 * h + p
                    if tap >= 27:
                        continue
                    a, b, e = tap // 9, tap // 3 % 3, tap % 3
                    into = w_two if layer else w_one
                    into[b, e * 128 : (e + 1) * 128, a * 128 : (a + 1) * 128] = plane.astype(BF16)
                    if layer:
                        a, b, e = 2 - a, 2 - b, 2 - e
                        w_back[b, e * 128 : (e + 1) * 128, a * 128 : (a + 1) * 128] = plane.T.astype(BF16)
    for r in range(COTS):
        for h in range(2):
            for p, plane in enumerate(planes(ROWS + r, h)):
                z = 2 * h + p
                cot[z * 128 : (z + 1) * 128, r * 128 : (r + 1) * 128] = plane

    for z in range(4):
        for r, value in enumerate(conv_plane(w_one, act, z, 6, 0)):
            row = 2 * chip - 2 + r
            inside = jnp.logical_and(row >= 0, row < 32)
            if r in (2, 3):
                pre[z * 128 : (z + 1) * 128, (r - 2) * 128 : (r - 1) * 128] = value
            kept = jnp.where(inside, jnp.where(value > 0, value, SLOPE * value), 0.0)
            hid[z * 128 : (z + 1) * 128, r * 128 : (r + 1) * 128] = kept.astype(BF16)

    held = {}
    for z in range(4):
        values = conv_plane(w_two, hid, z, 4, 0)
        for r, value in enumerate(values):
            at = (slice(z * 128, (z + 1) * 128), slice(r * 128, (r + 1) * 128))
            error = cot[at] * jnp.where(value > 0, 1.0, SLOPE)
            err[at] = error.astype(BF16)
            if r in (1, 2):
                put_errors(shifted, error, core, z, r - 1)
        own = jnp.where(core == 0, values[1], values[2])
        held[z % 2] = jnp.where(own > 0, own, SLOPE * own).reshape(16, 8, 128)
        if z % 2:
            low = low_half((16, 8, 128))
            half = slice((z // 2) * 8, (z // 2) * 8 + 8)
            for c, tile in enumerate((
                jnp.where(low, held[0], swap_halves(held[1])),
                jnp.where(low, swap_halves(held[0]), held[1]),
            )):
                out_tiles[:, c, half] = tile.astype(BF16)

    for x in range(4):
        for g in range(2):
            grads[x, 3, g * 7 + 6] = jnp.zeros((16, 128), BF16)
    tap_grad(shifted, hid, 1, total, grads, 1)

    for z in range(4):
        for r, value in enumerate(conv_plane(w_back, err, z, 2, 0)):
            slope = jnp.where(
                pre[z * 128 : (z + 1) * 128, r * 128 : (r + 1) * 128] > 0, 1.0, SLOPE
            )
            put_errors(shifted, value * slope, core, z, r)
    tap_grad(shifted, act, 2, total, grads, 0)


def compute(place, mine, other):
    vmem = pl.BlockSpec(memory_space=pltpu.VMEM)
    return pl.pallas_call(
        work,
        out_shape=(
            jax.ShapeDtypeStruct((16, 2, 16, 128), BF16),
            jax.ShapeDtypeStruct((4, 4, 14, 16, 128), BF16),
        ),
        in_specs=[pl.BlockSpec(memory_space=pltpu.SMEM), vmem, vmem],
        out_specs=(vmem, vmem),
        scratch_shapes=[
            pltpu.VMEM((512, 1024), BF16),
            pltpu.VMEM((512, 768), BF16),
            pltpu.VMEM((512, 512), BF16),
            pltpu.VMEM((512, 512), F32),
            pltpu.VMEM((3, 384, 384), BF16),
            pltpu.VMEM((3, 384, 384), BF16),
            pltpu.VMEM((3, 384, 384), BF16),
            pltpu.VMEM((512, 256), F32),
            pltpu.VMEM((192, 1024), BF16),
            pltpu.VMEM((192, 384), F32),
        ],
        compiler_params=pltpu.CompilerParams(vmem_limit_bytes=48 * 1024 * 1024),
        cost_estimate=pl.CostEstimate(flops=6_300_000_000, bytes_accessed=6_000_000, transcendentals=0),
        name="convolutions",
    )(place, mine, other)


def spread_rows(array, before, count):
    rows = jnp.transpose(array[0], (2, 1, 0, 3)).reshape(32, 16, 128)
    after = 2 * (15 + count) - 32 - before
    pairs = jnp.pad(rows, ((before, after), (0, 0), (0, 0))).reshape(15 + count, 2, 16, 128)
    return jnp.concatenate([pairs[j : j + 16] for j in range(count)], 1)


def own_taps(weight):
    rows = jnp.transpose(weight.reshape(27, 128, 4), (0, 2, 1))
    return jnp.pad(rows, ((0, 1), (0, 0), (0, 0))).reshape(7, 16, 128)


def on_device(activations, weight_one, weight_two, grad_out):
    core = lax.axis_index("c")
    chip = lax.axis_index(CHIPS)
    weights = jnp.concatenate([own_taps(weight_one), own_taps(weight_two)], 0)
    packed = jnp.concatenate(
        [
            spread_rows(activations, 3, 4),
            spread_rows(grad_out, 1, 2),
            jnp.broadcast_to(weights[None], (16, 14, 16, 128)),
        ],
        1,
    )
    mine = lax.all_to_all(packed, CHIPS, split_axis=0, concat_axis=0, tiled=True)
    other = lax.ppermute(mine, "c", [(0, 1), (1, 0)])
    place = jnp.stack([core, chip]).astype(jnp.int32)
    tiles, grads = compute(place, mine, other)

    parts = lax.all_to_all(grads.reshape(16, 14, 16, 128), ("x", "y"), split_axis=0, concat_axis=0, tiled=True)
    summed = parts.astype(F32).sum(0).astype(BF16)
    pieces = jnp.transpose(summed.reshape(14, 4, 4, 128), (1, 0, 2, 3)).reshape(1, 4, 56, 128)
    spread = jnp.broadcast_to(pieces, (4, 4, 56, 128)).reshape(16, 56, 128)
    depth = lax.all_to_all(spread, ("zh", "zl"), split_axis=0, concat_axis=0, tiled=True)
    piece = depth.astype(F32).sum(0).astype(BF16)
    every = lax.all_to_all(
        jnp.broadcast_to(piece[None], (4, 56, 128)), "y", split_axis=0, concat_axis=0, tiled=True
    )
    taps = jnp.transpose(every.reshape(4, 2, 7, 4, 128), (1, 0, 2, 3, 4)).reshape(2, 28, 4, 128)
    taps = jnp.transpose(taps[:, :27].astype(F32), (0, 1, 3, 2)).reshape(2, 3, 3, 3, 128, 4)

    rows = lax.all_to_all(tiles.reshape(32, 16, 128), FILT, split_axis=0, concat_axis=0, tiled=True)
    result = jnp.transpose(rows.reshape(32, 4, 4, 128), (2, 1, 0, 3))[None]
    return (result, taps[0], taps[1])


def solution(mesh):
    fine = Mesh(np.asarray(mesh.devices).reshape(4, 4, 2, 4, 4), ("zl", "x", "c", "zh", "y"))
    volumes = P(DP, FILT, None, None, None)
    filters = P(None, None, None, None, FILT)
    return jax.shard_map(
        on_device,
        mesh=fine,
        in_specs=(volumes, filters, filters, volumes),
        out_specs=(volumes, filters, filters),
        check_vma=False,
    )
```

time: 686 us -> 143 us (0.21)
  the two profiles are of different devices: /device:TPU:2 before, /device:TPU:1 now
where the time goes in v1:
time: 143 us
  blocking collectives  93 us (65%)
  starting transfers between devices  19 us (13%)
  waiting for transfers between devices  15.3 us (11%)
  Pallas kernels  8.29 us (6%)
  local copies, waits for them, and re-layouts  6.23 us (4%)
    all_to_all x1, blocking collectives, on_device(): lax.all_to_all(packed, CHIPS, split_axis=0, concat_axis=0, tiled=True)  49.3 us
    all_to_all x1, blocking collectives, on_device(): lax.all_to_all(spread, ('zh', 'zl'), split_axis=0, concat_axis=0, tiled=T...  24.6 us
    all_to_all x1, blocking collectives, on_device(): lax.all_to_all(grads.reshape(16, 14, 16, 128), ('x', 'y'), split_axis=0,...  19.1 us
    all_to_all x1, starting transfers between devices, on_device(): lax.all_to_all(tiles.reshape(32, 16, 128), FILT, split_axis=0, concat_axi...  11.8 us
    all_to_all x1, waiting for transfers between devices, on_device(): lax.all_to_all(tiles.reshape(32, 16, 128), FILT, split_axis=0, concat_axi...  8.5 us
    pallas_call x1, Pallas kernels, compute(): pl.pallas_call(work, out_shape=(jax.ShapeDtypeStruct((16, 2, 16, 128), BF...  8.29 us
    ppermute x1, starting transfers between devices, on_device(): other = lax.ppermute(mine, 'c', [(0, 1), (1, 0)])  3.94 us
    all_to_all x1, waiting for transfers between devices, on_device(): lax.all_to_all(jnp.broadcast_to(piece[None], (4, 56, 128)), 'y', split_ax...  3.69 us
  transfers between devices with their start and end apart: 3, of which 3 were waited for; matrix products, arithmetic and copies ran while one was open for 1% of the time, Pallas kernels for 0%

profile of v1, /device:TPU:1, one launch (start us, length us, event | category | flops | bytes accessed | tf_op | source)
XLA Modules:
  0.0 142.9 jit_solution(17147567078223923669)
XLA Ops:
  0.6 0.8 pad.17
  1.4 0.8 pad.18
  2.2 0.9 copy.41
  3.1 0.9 copy.46
  4.0 0.1 pad_slice_fusion
  4.1 0.1 copy.48
  4.1 0.1 copy.47
  4.2 0.1 pad_slice_fusion.2
  4.3 0.1 copy.45
  4.4 0.1 copy.43
  4.4 0.1 copy.44
  4.5 0.1 copy.42
  4.7 0.2 broadcast_dynamic-update-slice_fusion
  4.9 49.3 %all_to_all.25.mine = bf16[16,26,16,128]{3,2,1,0:T(8,128)(2,1)S(1)} all-to-all(bf16[16,26,16,128]{3,2,1,0:T(8,128)(2,1)S(1)} %broadcast_dynamic-update-slice_fusion), channel_id=1, replica_groups=mesh['zl'=4,'x'=4,'c'=2,'zh'=4,'y'=4] {'zl','x'}, dimensions={0} | all-to-all | bytes 3407872 | tf_op jit(solution)/shard_map/all_to_all | solution.py:230
  54.2 3.9 %collective-permute-start = (bf16[16,26,16,128]{3,2,1,0:T(8,128)(2,1)S(1)}, bf16[16,26,16,128]{3,2,1,0:T(8,128)(2,1)S(1)}, u32[]{:S(2)}, u32[]{:S(2)}) collective-permute-start(bf16[16,26,16,128]{3,2,1,0:T(8,128)(2,1)S(1)} %all_to_all.25.mine), channel_id=1, source_target_pairs={{0,16},{16,0},{1,17},{17,1},{2,18},{18,2},{3,19},{19,3},{4,20},{20... | collective-permute-start | bytes 5111816 | tf_op jit(solution)/shard_map/ppermute | solution.py:231
  58.2 0.1 pad_add_fusion.place
  58.2 3.1 %collective-permute-done.other = bf16[16,26,16,128]{3,2,1,0:T(8,128)(2,1)S(1)} collective-permute-done((bf16[16,26,16,128]{3,2,1,0:T(8,128)(2,1)S(1)}, bf16[16,26,16,128]{3,2,1,0:T(8,128)(2,1)S(1)}, u32[]{:S(2)}, u32[]{:S(2)}) %collective-permute-start) | collective-permute-done | bytes 1703968 | tf_op jit(solution)/shard_map/ppermute | solution.py:231
  61.4 8.3 %convolutions.1 = (bf16[16,2,16,128]{3,2,1,0:T(8,128)(2,1)}, bf16[4,4,14,16,128]{4,3,2,1,0:T(8,128)(2,1)S(1)}) custom-call(s32[2]{0:T(128)S(1)} %pad_add_fusion.place, bf16[16,26,16,128]{3,2,1,0:T(8,128)(2,1)S(1)} %all_to_all.25.mine, bf16[16,26,16,128]{3,2,1,0:T(8,128)(2,1)S(1)} %collective-permute-done.other), custom_call_target="tpu_custom_call" | custom-call | flops 6300000256 | bytes 6000000 | tf_op jit(solution)/shard_map/convolutions/pallas_call | solution.py:180
  69.7 19.1 %all_to_all.26 = bf16[16,14,16,128]{3,2,1,0:T(8,128)(2,1)S(1)} all-to-all(bf16[16,14,16,128]{3,2,1,0:T(8,128)(2,1)S(1)} %bitcast.46), channel_id=1, replica_groups=mesh['zl'=4,'x'=4,'c'=2,'zh'=4,'y'=4] {'x','y'}, dimensions={0} | all-to-all | bytes 1835008 | tf_op jit(solution)/shard_map/all_to_all | solution.py:235
  88.8 0.1 reduce_sum.24
  89.0 24.6 %all_to_all.27 = bf16[16,56,128]{2,1,0:T(8,128)(2,1)S(1)} all-to-all(bf16[16,56,128]{2,1,0:T(8,128)(2,1)S(1)} %bitcast.47), channel_id=1, replica_groups=mesh['zl'=4,'x'=4,'c'=2,'zh'=4,'y'=4] {'zh','zl'}, dimensions={0} | all-to-all | bytes 458752 | tf_op jit(solution)/shard_map/all_to_all | solution.py:239
  113.6 11.8 %all-to-all-start.1 = ((bf16[32,16,128]{2,1,0:T(8,128)(2,1)}), bf16[32,16,128]{2,1,0:T(8,128)(2,1)S(1)}, u32[]{:S(2)}, u32[]{:S(2)}) async-start(bf16[32,16,128]{2,1,0:T(8,128)(2,1)} %bitcast.20), calls=%async_computation.1 | async-start | bytes 262144 | tf_op jit(solution)/shard_map/all_to_all | solution.py:247
  125.4 8.5 %all-to-all-done.1 = bf16[32,16,128]{2,1,0:T(8,128)(2,1)S(1)} async-done(((bf16[32,16,128]{2,1,0:T(8,128)(2,1)}), bf16[32,16,128]{2,1,0:T(8,128)(2,1)S(1)}, u32[]{:S(2)}, u32[]{:S(2)}) %all-to-all-start.1) | async-done | bytes 131104 | tf_op jit(solution)/shard_map/all_to_all | solution.py:247
  133.9 0.6 broadcast_in_dim.26
  134.5 3.3 %all-to-all-start.4 = ((bf16[4,56,128]{2,1,0:T(8,128)(2,1)}), bf16[4,56,128]{2,1,0:T(8,128)(2,1)S(1)}, u32[]{:S(2)}, u32[]{:S(2)}) async-start(bf16[4,56,128]{2,1,0:T(8,128)(2,1)} %broadcast_in_dim.26), calls=%async_computation.4 | async-start | bytes 114688 | tf_op jit(solution)/shard_map/all_to_all | solution.py:241
  137.9 0.7 copy.52
  138.5 3.7 %all-to-all-done.4 = bf16[4,56,128]{2,1,0:T(8,128)(2,1)S(1)} async-done(((bf16[4,56,128]{2,1,0:T(8,128)(2,1)}), bf16[4,56,128]{2,1,0:T(8,128)(2,1)S(1)}, u32[]{:S(2)}, u32[]{:S(2)}) %all-to-all-start.4) | async-done | bytes 57376 | tf_op jit(solution)/shard_map/all_to_all | solution.py:241
  142.3 0.6 fusion
  (13 shorter events, 0.3 us)
Async XLA Ops:
  54.2 7.1 %collective-permute-start = (bf16[16,26,16,128]{3,2,1,0:T(8,128)(2,1)S(1)}, bf16[16,26,16,128]{3,2,1,0:T(8,128)(2,1)S(1)}, u32[]{:S(2)}, u32[]{:S(2)}) collective-permute-start(bf16[16,26,16,128]{3,2,1,0:T(8,128)(2,1)S(1)} %all_to_all.25.mine), channel_id=1, source_target_pairs={{0,16},{16,0},{1,17},{17,1},{2,18},{18,2},{3,19},{19,3},{4,20},{20... | collective-permute-start | bytes 5111816 | tf_op jit(solution)/shard_map/ppermute | solution.py:231
  113.6 20.3 %all-to-all-start.1 = ((bf16[32,16,128]{2,1,0:T(8,128)(2,1)}), bf16[32,16,128]{2,1,0:T(8,128)(2,1)S(1)}, u32[]{:S(2)}, u32[]{:S(2)}) async-start(bf16[32,16,128]{2,1,0:T(8,128)(2,1)} %bitcast.20), calls=%async_computation.1 | async-start | bytes 262144 | tf_op jit(solution)/shard_map/all_to_all | solution.py:247
  134.5 7.7 %all-to-all-start.4 = ((bf16[4,56,128]{2,1,0:T(8,128)(2,1)}), bf16[4,56,128]{2,1,0:T(8,128)(2,1)S(1)}, u32[]{:S(2)}, u32[]{:S(2)}) async-start(bf16[4,56,128]{2,1,0:T(8,128)(2,1)} %broadcast_in_dim.26), calls=%async_computation.4 | async-start | bytes 114688 | tf_op jit(solution)/shard_map/all_to_all | solution.py:241

commit v2 on v1

--- a/solution.py
+++ b/solution.py
@@ -23,11 +23,9 @@
     return pltpu.roll(tiles, 4, tiles.ndim - 2)
 
 
-def merge(mine, other, core):
-    low = low_half(mine.shape)
-    first = jnp.where(low, mine, swap_halves(other))
-    second = jnp.where(low, swap_halves(mine), other)
-    return [pltpu.roll(plane, 4 * core, plane.ndim - 2) for plane in (first, second)]
+def merge(even, odd):
+    low = low_half(even.shape)
+    return jnp.where(low, even, swap_halves(odd)), jnp.where(low, swap_halves(even), odd)
 
 
 def shift_lanes(block, by):
@@ -98,25 +96,37 @@
 
 
 def work(
-    place, mine, other, out_tiles, grads,
-    act, hid, err, cot, w_one, w_two, w_back, pre, shifted, total,
+    place, mine, other, mine_taps, other_taps, out_tiles, grads,
+    act, hid, err, cot, w_one, w_two, w_back, pre, shifted, total, tiles, sent,
 ):
     core, chip = place[0], place[1]
 
-    def planes(step, h):
-        one = mine[:, step].astype(F32).reshape(16, 2, 8, 128)[:, h]
-        two = other[:, step].astype(F32).reshape(16, 2, 8, 128)[:, h]
-        return [plane.reshape(128, 128) for plane in merge(one, two, core)]
+    even_core = lax.broadcast(core, (16, 2, 8, 128)) == 0
+
+    def load(one, two):
+        one = one.astype(F32).reshape(16, 2, 8, 128)
+        two = two.astype(F32).reshape(16, 2, 8, 128)
+        return jnp.where(even_core, one, two), jnp.where(even_core, two, one)
+
+    def filters(source, step):
+        return jnp.stack([source[x, zl, step] for zl in range(4) for x in range(4)])
+
+    def planes(one, two, h):
+        merged = merge(one[:, h], two[:, h])
+        return [plane.reshape(128, 128) for plane in merged]
 
     for r in range(ROWS):
+        one, two = load(mine[:, r], other[:, r])
         for h in range(2):
-            for p, plane in enumerate(planes(r, h)):
+            for p, plane in enumerate(planes(one, two, h)):
                 z = 2 * h + p
                 act[z * 128 : (z + 1) * 128, r * 128 : (r + 1) * 128] = plane.astype(BF16)
     for layer in range(2):
         for step in range(7):
+            at = layer * 7 + step
+            one, two = load(filters(mine_taps, at), filters(other_taps, at))
             for h in range(2):
-                for p, plane in enumerate(planes(ROWS + COTS + layer * 7 + step, h)):
+                for p, plane in enumerate(planes(one, two, h)):
                     tap = 4 * step + 2 * h + p
                     if tap >= 27:
                         continue
@@ -127,8 +137,9 @@
                         a, b, e = 2 - a, 2 - b, 2 - e
                         w_back[b, e * 128 : (e + 1) * 128, a * 128 : (a + 1) * 128] = plane.T.astype(BF16)
     for r in range(COTS):
+        one, two = load(mine[:, ROWS + r], other[:, ROWS + r])
         for h in range(2):
-            for p, plane in enumerate(planes(ROWS + r, h)):
+            for p, plane in enumerate(planes(one, two, h)):
                 z = 2 * h + p
                 cot[z * 128 : (z + 1) * 128, r * 128 : (r + 1) * 128] = plane
 
@@ -154,12 +165,14 @@
         held[z % 2] = jnp.where(own > 0, own, SLOPE * own).reshape(16, 8, 128)
         if z % 2:
             low = low_half((16, 8, 128))
-            half = slice((z // 2) * 8, (z // 2) * 8 + 8)
+            rows = slice((z // 2) * 8, (z // 2) * 8 + 8)
             for c, tile in enumerate((
                 jnp.where(low, held[0], swap_halves(held[1])),
                 jnp.where(low, swap_halves(held[0]), held[1]),
             )):
-                out_tiles[:, c, half] = tile.astype(BF16)
+                tiles[:, c, rows] = tile.astype(BF16)
+    send = pltpu.make_async_copy(tiles, out_tiles, sent)
+    send.start()
 
     for x in range(4):
         for g in range(2):
@@ -173,9 +186,10 @@
             )
             put_errors(shifted, value * slope, core, z, r)
     tap_grad(shifted, act, 2, total, grads, 0)
-
-
-def compute(place, mine, other):
+    send.wait()
+
+
+def compute(place, *arrays):
     vmem = pl.BlockSpec(memory_space=pltpu.VMEM)
     return pl.pallas_call(
         work,
@@ -183,8 +197,8 @@
             jax.ShapeDtypeStruct((16, 2, 16, 128), BF16),
             jax.ShapeDtypeStruct((4, 4, 14, 16, 128), BF16),
         ),
-        in_specs=[pl.BlockSpec(memory_space=pltpu.SMEM), vmem, vmem],
-        out_specs=(vmem, vmem),
+        in_specs=[pl.BlockSpec(memory_space=pltpu.SMEM), vmem, vmem, vmem, vmem],
+        out_specs=(pl.BlockSpec(memory_space=pltpu.HBM), vmem),
         scratch_shapes=[
             pltpu.VMEM((512, 1024), BF16),
             pltpu.VMEM((512, 768), BF16),
@@ -196,57 +210,112 @@
             pltpu.VMEM((512, 256), F32),
             pltpu.VMEM((192, 1024), BF16),
             pltpu.VMEM((192, 384), F32),
+            pltpu.VMEM((16, 2, 16, 128), BF16),
+            pltpu.SemaphoreType.DMA,
         ],
         compiler_params=pltpu.CompilerParams(vmem_limit_bytes=48 * 1024 * 1024),
         cost_estimate=pl.CostEstimate(flops=6_300_000_000, bytes_accessed=6_000_000, transcendentals=0),
         name="convolutions",
-    )(place, mine, other)
-
-
-def spread_rows(array, before, count):
-    rows = jnp.transpose(array[0], (2, 1, 0, 3)).reshape(32, 16, 128)
-    after = 2 * (15 + count) - 32 - before
-    pairs = jnp.pad(rows, ((before, after), (0, 0), (0, 0))).reshape(15 + count, 2, 16, 128)
-    return jnp.concatenate([pairs[j : j + 16] for j in range(count)], 1)
+    )(place, *arrays)
+
+
+def pack_taps(one, two, out, near, sems):
+    copies = [pltpu.make_async_copy(taps, near.at[n], sems.at[n]) for n, taps in enumerate((one, two))]
+    for copy in copies:
+        copy.start()
+    for layer, copy in enumerate(copies):
+        copy.wait()
+        for step in range(7):
+            parts = [near[layer, 4 * step + t].astype(F32) for t in range(min(4, 27 - 4 * step))]
+            if len(parts) == 3:
+                parts.append(jnp.zeros((4, 128), F32))
+            tile = jnp.concatenate(parts, 0).astype(BF16)
+            for zl in range(4):
+                out[zl, layer * 7 + step] = tile
+
+
+def pack_rows(volume, cotangent, after, out):
+    for source, start, halo, count in ((volume, 0, 3, ROWS), (cotangent, ROWS, 1, COTS)):
+        planes = [source[ch, z].astype(F32) for z in range(4) for ch in range(4)]
+        rows = jnp.swapaxes(jnp.stack(planes), 0, 1).astype(BF16)
+        for chip in range(16):
+            for r in range(count):
+                row = 2 * chip + r - halo
+                if 0 <= row < 32:
+                    out[chip, start + r] = rows[row]
+                else:
+                    out[chip, start + r] = jnp.zeros((16, 128), BF16)
+
+
+def sum_pieces(pieces, tiles, total, kept):
+    total[...] = pieces[...].astype(F32).sum(0).astype(BF16)
+
+
+VMEM = pl.BlockSpec(memory_space=pltpu.VMEM)
+HBM = pl.BlockSpec(memory_space=pltpu.HBM)
+
+
+def on_chip(kernel, shapes, specs, *arrays, out_specs=VMEM, **options):
+    return pl.pallas_call(
+        kernel,
+        out_shape=shapes,
+        in_specs=specs,
+        out_specs=out_specs,
+        compiler_params=pltpu.CompilerParams(vmem_limit_bytes=24 * 1024 * 1024),
+        **options,
+    )(*arrays)
 
 
 def own_taps(weight):
-    rows = jnp.transpose(weight.reshape(27, 128, 4), (0, 2, 1))
-    return jnp.pad(rows, ((0, 1), (0, 0), (0, 0))).reshape(7, 16, 128)
+    return jnp.transpose(weight.reshape(27, 128, 4), (0, 2, 1))
+
+
+def exchange(array, axis):
+    return lax.all_to_all(array, axis, split_axis=0, concat_axis=0, tiled=True)
 
 
 def on_device(activations, weight_one, weight_two, grad_out):
     core = lax.axis_index("c")
     chip = lax.axis_index(CHIPS)
-    weights = jnp.concatenate([own_taps(weight_one), own_taps(weight_two)], 0)
-    packed = jnp.concatenate(
-        [
-            spread_rows(activations, 3, 4),
-            spread_rows(grad_out, 1, 2),
-            jnp.broadcast_to(weights[None], (16, 14, 16, 128)),
-        ],
-        1,
+    taps = on_chip(
+        pack_taps, jax.ShapeDtypeStruct((4, 14, 16, 128), BF16), [HBM, HBM],
+        own_taps(weight_one), own_taps(weight_two),
+        scratch_shapes=[pltpu.VMEM((2, 27, 4, 128), BF16), pltpu.SemaphoreType.DMA((2,))],
+        name="pack_taps",
     )
-    mine = lax.all_to_all(packed, CHIPS, split_axis=0, concat_axis=0, tiled=True)
-    other = lax.ppermute(mine, "c", [(0, 1), (1, 0)])
+    line = exchange(taps, "zl")
+    packed = on_chip(
+        pack_rows, jax.ShapeDtypeStruct((16, ROWS + COTS, 16, 128), BF16), [VMEM, VMEM, HBM],
+        activations[0], grad_out[0], line, name="pack_rows",
+    )
+    mine = exchange(packed, CHIPS)
+    mine_taps = lax.all_gather(line[None], "x", axis=0, tiled=True)
+    swap = [(0, 1), (1, 0)]
+    other, other_taps = lax.ppermute(mine, "c", swap), lax.ppermute(mine_taps, "c", swap)
     place = jnp.stack([core, chip]).astype(jnp.int32)
-    tiles, grads = compute(place, mine, other)
-
-    parts = lax.all_to_all(grads.reshape(16, 14, 16, 128), ("x", "y"), split_axis=0, concat_axis=0, tiled=True)
+    tiles, grads = compute(place, mine, other, mine_taps, other_taps)
+
+    parts = exchange(grads.reshape(16, 14, 16, 128), ("x", "y"))
     summed = parts.astype(F32).sum(0).astype(BF16)
     pieces = jnp.transpose(summed.reshape(14, 4, 4, 128), (1, 0, 2, 3)).reshape(1, 4, 56, 128)
     spread = jnp.broadcast_to(pieces, (4, 4, 56, 128)).reshape(16, 56, 128)
-    depth = lax.all_to_all(spread, ("zh", "zl"), split_axis=0, concat_axis=0, tiled=True)
-    piece = depth.astype(F32).sum(0).astype(BF16)
-    every = lax.all_to_all(
-        jnp.broadcast_to(piece[None], (4, 56, 128)), "y", split_axis=0, concat_axis=0, tiled=True
+    depth = exchange(spread, ("zh", "zl"))
+
+    piece, tiles = on_chip(
+        sum_pieces,
+        (jax.ShapeDtypeStruct((56, 128), BF16), jax.ShapeDtypeStruct(tiles.shape, BF16)),
+        [VMEM, HBM], depth, tiles,
+        out_specs=(VMEM, HBM),
+        input_output_aliases={1: 1},
+        name="sum_pieces",
     )
-    taps = jnp.transpose(every.reshape(4, 2, 7, 4, 128), (1, 0, 2, 3, 4)).reshape(2, 28, 4, 128)
-    taps = jnp.transpose(taps[:, :27].astype(F32), (0, 1, 3, 2)).reshape(2, 3, 3, 3, 128, 4)
-
-    rows = lax.all_to_all(tiles.reshape(32, 16, 128), FILT, split_axis=0, concat_axis=0, tiled=True)
+    every = lax.all_gather(piece[None], "y", axis=0, tiled=True)
+    found = jnp.transpose(every.reshape(4, 2, 7, 4, 128), (1, 0, 2, 3, 4)).reshape(2, 28, 4, 128)
+    found = jnp.transpose(found[:, :27].astype(F32), (0, 1, 3, 2)).reshape(2, 3, 3, 3, 128, 4)
+
+    rows = exchange(tiles.reshape(32, 16, 128), FILT)
     result = jnp.transpose(rows.reshape(32, 4, 4, 128), (2, 1, 0, 3))[None]
-    return (result, taps[0], taps[1])
+    return (result, found[0], found[1])
 
 
 def solution(mesh):

time: 143 us -> 129 us (0.902)
  the two profiles are of different devices: /device:TPU:1 before, /device:TPU:2 now
where the time goes in v2:
time: 129 us
  blocking collectives  95.5 us (74%)
  starting transfers between devices  17.4 us (13%)
  Pallas kernels  9.97 us (8%)
  local copies, waits for them, and re-layouts  2.92 us (2%)
  waiting for transfers between devices  1.94 us (2%)
    all_to_all x3, blocking collectives, exchange(): return lax.all_to_all(array, axis, split_axis=0, concat_axis=0, tiled=True)  65 us
    all_gather x1, blocking collectives, on_device(): mine_taps = lax.all_gather(line[None], 'x', axis=0, tiled=True)  18.6 us
    all_to_all x2, starting transfers between devices, exchange(): return lax.all_to_all(array, axis, split_axis=0, concat_axis=0, tiled=True)  13.1 us
    all_gather x1, blocking collectives, on_device(): every = lax.all_gather(piece[None], 'y', axis=0, tiled=True)  11.9 us
    pallas_call x1, Pallas kernels, compute(): pl.pallas_call(work, out_shape=(jax.ShapeDtypeStruct((16, 2, 16, 128), BF...  8.86 us
  transfers between devices with their start and end apart: 4, of which 1 were waited for; matrix products, arithmetic and copies ran while one was open for 1% of the time, Pallas kernels for 0%

profile of v2, /device:TPU:2, one launch (start us, length us, event | category | flops | bytes accessed | tf_op | source)
XLA Modules:
  0.0 128.6 jit_solution(2872306857442740553)
XLA Ops:
  0.6 0.0 copy-start.2
  0.6 0.7 copy-done.2
  1.4 0.0 copy-start.3
  1.4 0.7 copy-done.3
  2.1 0.1 pack_taps.1
  2.2 0.0 copy-start
  2.2 0.0 copy-start.1
  2.2 14.0 %all_to_all.25.after = bf16[4,14,16,128]{3,2,1,0:T(8,128)(2,1)S(1)} all-to-all(bf16[4,14,16,128]{3,2,1,0:T(8,128)(2,1)S(1)} %pack_taps.1), channel_id=1, replica_groups=mesh['zl'=4,'x'=4,'c'=2,'zh'=4,'y'=4] {'zl'}, dimensions={0} | all-to-all | bytes 458752 | tf_op jit(solution)/shard_map/all_to_all | solution.py:274
  16.2 0.0 copy-done
  16.2 0.0 copy-done.1
  16.2 1.0 pack_rows.1
  17.2 5.7 %all-to-all-start.1 = ((bf16[16,12,16,128]{3,2,1,0:T(8,128)(2,1)}), bf16[16,12,16,128]{3,2,1,0:T(8,128)(2,1)S(1)}, u32[]{:S(2)}, u32[]{:S(2)}) async-start(bf16[16,12,16,128]{3,2,1,0:T(8,128)(2,1)} %pack_rows.1), calls=%async_computation.1 | async-start | bytes 1572864 | tf_op jit(solution)/shard_map/all_to_all | solution.py:274
  23.0 18.6 %all-gather = bf16[16,14,16,128]{3,2,1,0:T(8,128)(2,1)S(1)} all-gather(bf16[4,14,16,128]{3,2,1,0:T(8,128)(2,1)S(1)} %all_to_all.25.after), channel_id=2, replica_groups=mesh['zl'=4,'x'=4,'c'=2,'zh'=4,'y'=4] {'x'}, dimensions={0}, use_global_device_ids=true | all-gather | bytes 1146880 | tf_op jit(solution)/shard_map/all_gather | solution.py:292
  41.6 1.9 %collective-permute-start.1 = (bf16[4,4,14,16,128]{4,3,2,1,0:T(8,128)(2,1)S(1)}, bf16[4,4,14,16,128]{4,3,2,1,0:T(8,128)(2,1)S(1)}, u32[]{:S(2)}, u32[]{:S(2)}) collective-permute-start(bf16[4,4,14,16,128]{4,3,2,1,0:T(8,128)(2,1)S(1)} %bitcast.32), channel_id=1, source_target_pairs={{0,16},{16,0},{1,17},{17,1},{2,18},{18,2},{3,19},{19,3},{4,20},{20... | collective-permute-start | bytes 2752520 | tf_op jit(solution)/shard_map/ppermute | solution.py:294
  43.5 0.0 all-to-all-done.1.mine
  43.5 2.4 %collective-permute-start = (bf16[16,12,16,128]{3,2,1,0:T(8,128)(2,1)S(1)}, bf16[16,12,16,128]{3,2,1,0:T(8,128)(2,1)}, u32[]{:S(2)}, u32[]{:S(2)}) collective-permute-start(bf16[16,12,16,128]{3,2,1,0:T(8,128)(2,1)S(1)} %all-to-all-done.1.mine), channel_id=1, source_target_pairs={{0,16},{16,0},{1,17},{17,1},{2,18},{18,2},{3,19},{19,3},{4,20},{20... | collective-permute-start | bytes 2359304 | tf_op jit(solution)/shard_map/ppermute | solution.py:294
  46.0 0.1 pad_add_fusion.place
  46.0 0.0 collective-permute-done.1.other_taps
  46.0 1.9 %collective-permute-done.other = bf16[16,12,16,128]{3,2,1,0:T(8,128)(2,1)} collective-permute-done((bf16[16,12,16,128]{3,2,1,0:T(8,128)(2,1)S(1)}, bf16[16,12,16,128]{3,2,1,0:T(8,128)(2,1)}, u32[]{:S(2)}, u32[]{:S(2)}) %collective-permute-start) | collective-permute-done | bytes 786464 | tf_op jit(solution)/shard_map/ppermute | solution.py:294
  48.0 8.9 %convolutions.1 = (bf16[16,2,16,128]{3,2,1,0:T(8,128)(2,1)}, bf16[4,4,14,16,128]{4,3,2,1,0:T(8,128)(2,1)S(1)}) custom-call(s32[2]{0:T(128)S(1)} %pad_add_fusion.place, bf16[16,12,16,128]{3,2,1,0:T(8,128)(2,1)S(1)} %all-to-all-done.1.mine, bf16[16,12,16,128]{3,2,1,0:T(8,128)(2,1)} %collective-permute-done.other, bf16[4,4,14,16,128]{4,3,2,1,0:T(8,128)(2,1)S(1)} %bitcast.33, ...), custom_call_target="tpu_custom_call" | custom-call | flops 6300000256 | bytes 6000000 | tf_op jit(solution)/shard_map/convolutions/pallas_call | solution.py:194
  56.8 21.0 %all_to_all.26 = bf16[16,14,16,128]{3,2,1,0:T(8,128)(2,1)S(1)} all-to-all(bf16[16,14,16,128]{3,2,1,0:T(8,128)(2,1)S(1)} %bitcast.31), channel_id=1, replica_groups=mesh['zl'=4,'x'=4,'c'=2,'zh'=4,'y'=4] {'x','y'}, dimensions={0} | all-to-all | bytes 1835008 | tf_op jit(solution)/shard_map/all_to_all | solution.py:274
  77.9 0.1 reduce_sum.12
  78.1 29.9 %all_to_all.27.pieces = bf16[16,56,128]{2,1,0:T(8,128)(2,1)S(1)} all-to-all(bf16[16,56,128]{2,1,0:T(8,128)(2,1)S(1)} %bitcast.38), channel_id=1, replica_groups=mesh['zl'=4,'x'=4,'c'=2,'zh'=4,'y'=4] {'zh','zl'}, dimensions={0} | all-to-all | bytes 458752 | tf_op jit(solution)/shard_map/all_to_all | solution.py:274
  108.0 7.3 %all-to-all-start.4 = ((bf16[32,16,128]{2,1,0:T(8,128)(2,1)}), bf16[32,16,128]{2,1,0:T(8,128)(2,1)S(1)}, u32[]{:S(2)}, u32[]{:S(2)}) async-start(bf16[32,16,128]{2,1,0:T(8,128)(2,1)} %bitcast.14), calls=%async_computation.4 | async-start | bytes 262144 | tf_op jit(solution)/shard_map/all_to_all | solution.py:274
  115.3 11.9 %all-gather.1 = bf16[224,128]{1,0:T(8,128)(2,1)S(1)} all-gather(bf16[56,128]{1,0:T(8,128)(2,1)S(1)} %get-tuple-element.10), channel_id=3, replica_groups=mesh['zl'=4,'x'=4,'c'=2,'zh'=4,'y'=4] {'y'}, dimensions={0}, use_global_device_ids=true | all-gather | bytes 71680 | tf_op jit(solution)/shard_map/all_gather | solution.py:312
  127.3 0.6 fusion
  127.9 0.0 all-to-all-done.4
  128.0 0.7 copy.18
  (6 shorter events, 0.2 us)
Async XLA Ops:
  0.6 0.7 copy-start.2
  1.4 0.7 copy-start.3
  2.2 14.0 %copy-start = (bf16[1,4,4,32,128]{4,3,2,1,0:T(8,128)(2,1)S(1)}, bf16[1,4,4,32,128]{4,3,2,1,0:T(8,128)(2,1)}, u32[]{:S(2)}) copy-start(bf16[1,4,4,32,128]{4,3,2,1,0:T(8,128)(2,1)} %param.4) | copy-start | bytes 393220
  2.2 14.0 %copy-start.1 = (bf16[1,4,4,32,128]{4,3,2,1,0:T(8,128)(2,1)S(1)}, bf16[1,4,4,32,128]{4,3,2,1,0:T(8,128)(2,1)}, u32[]{:S(2)}) copy-start(bf16[1,4,4,32,128]{4,3,2,1,0:T(8,128)(2,1)} %param.7) | copy-start | bytes 393220
  17.2 26.3 %all-to-all-start.1 = ((bf16[16,12,16,128]{3,2,1,0:T(8,128)(2,1)}), bf16[16,12,16,128]{3,2,1,0:T(8,128)(2,1)S(1)}, u32[]{:S(2)}, u32[]{:S(2)}) async-start(bf16[16,12,16,128]{3,2,1,0:T(8,128)(2,1)} %pack_rows.1), calls=%async_computation.1 | async-start | bytes 1572864 | tf_op jit(solution)/shard_map/all_to_all | solution.py:274
  41.6 4.4 %collective-permute-start.1 = (bf16[4,4,14,16,128]{4,3,2,1,0:T(8,128)(2,1)S(1)}, bf16[4,4,14,16,128]{4,3,2,1,0:T(8,128)(2,1)S(1)}, u32[]{:S(2)}, u32[]{:S(2)}) collective-permute-start(bf16[4,4,14,16,128]{4,3,2,1,0:T(8,128)(2,1)S(1)} %bitcast.32), channel_id=1, source_target_pairs={{0,16},{16,0},{1,17},{17,1},{2,18},{18,2},{3,19},{19,3},{4,20},{20... | collective-permute-start | bytes 2752520 | tf_op jit(solution)/shard_map/ppermute | solution.py:294
  43.5 4.4 %collective-permute-start = (bf16[16,12,16,128]{3,2,1,0:T(8,128)(2,1)S(1)}, bf16[16,12,16,128]{3,2,1,0:T(8,128)(2,1)}, u32[]{:S(2)}, u32[]{:S(2)}) collective-permute-start(bf16[16,12,16,128]{3,2,1,0:T(8,128)(2,1)S(1)} %all-to-all-done.1.mine), channel_id=1, source_target_pairs={{0,16},{16,0},{1,17},{17,1},{2,18},{18,2},{3,19},{19,3},{4,20},{20... | collective-permute-start | bytes 2359304 | tf_op jit(solution)/shard_map/ppermute | solution.py:294
  108.0 19.9 %all-to-all-start.4 = ((bf16[32,16,128]{2,1,0:T(8,128)(2,1)}), bf16[32,16,128]{2,1,0:T(8,128)(2,1)S(1)}, u32[]{:S(2)}, u32[]{:S(2)}) async-start(bf16[32,16,128]{2,1,0:T(8,128)(2,1)} %bitcast.14), calls=%async_computation.4 | async-start | bytes 262144 | tf_op jit(solution)/shard_map/all_to_all | solution.py:274

commit v3 on v2

--- a/solution.py
+++ b/solution.py
@@ -23,6 +23,13 @@
     return pltpu.roll(tiles, 4, tiles.ndim - 2)
 
 
+def channel_order():
+    row = lax.broadcasted_iota(jnp.int32, (128, 128), 0)
+    column = lax.broadcasted_iota(jnp.int32, (128, 128), 1)
+    core, x, zl, last = column // 64, column // 16 % 4, column // 4 % 4, column % 4
+    return jnp.where(row == 32 * zl + 8 * x + 4 * core + last, 1.0, 0.0).astype(BF16)
+
+
 def merge(even, odd):
     low = low_half(even.shape)
     return jnp.where(low, even, swap_halves(odd)), jnp.where(low, swap_halves(even), odd)
@@ -37,15 +44,14 @@
 def conv_plane(weights, source, depth, rows, first_row):
     low, high = max(depth - 1, 0), min(depth + 1, 3)
     taps = slice((low - depth + 1) * 128, (high - depth + 2) * 128)
-    total = None
-    for b in range(3):
-        lanes = slice((first_row + b) * 128, (first_row + b + rows) * 128)
-        part = jnp.dot(
-            weights[b, :, taps],
-            source[low * 128 : (high + 1) * 128, lanes],
-            preferred_element_type=F32,
-        )
-        total = part if total is None else total + part
+    total = jnp.dot(
+        jnp.concatenate([weights[b, :, taps] for b in range(3)], 1),
+        jnp.concatenate([
+            source[low * 128 : (high + 1) * 128, (first_row + b) * 128 : (first_row + b + rows) * 128]
+            for b in range(3)
+        ], 0),
+        preferred_element_type=F32,
+    )
     out = []
     for r in range(rows):
         block = total[:, r * 128 : (r + 1) * 128]
@@ -55,18 +61,8 @@
     return out
 
 
-def own_rows(block, core):
-    tiles = pltpu.roll(block.reshape(4, 4, 8, 128), (8 - 4 * core) % 8, 2)
-    pairs = []
-    for x in range(4):
-        for zl in (0, 2):
-            one, two = tiles[zl, x], tiles[zl + 1, x]
-            pairs.append(jnp.where(low_half(one.shape), one, swap_halves(two)))
-    return jnp.concatenate(pairs, 0)
-
-
 def put_errors(shifted, block, core, depth, row):
-    own = own_rows(block, core)
+    own = jnp.where(core == 0, block[:64], block[64:])
     lanes = slice((depth * 2 + row) * 128, (depth * 2 + row + 1) * 128)
     shifted[0:64, lanes] = shift_lanes(own, -1).astype(BF16)
     shifted[64:128, lanes] = own.astype(BF16)
@@ -95,53 +91,50 @@
                     ].astype(BF16)
 
 
+def planes(group, h):
+    halves = [[tile.astype(F32)[h * 8 : h * 8 + 8] for tile in line] for line in group]
+    even = jnp.stack([line[zl] for line in halves for zl in (0, 2)])
+    odd = jnp.stack([line[zl] for line in halves for zl in (1, 3)])
+    return [plane.reshape(64, 128).astype(BF16) for plane in merge(even, odd)]
+
+
+def place_half(side, rows, taps, act, cot, w_one, w_two):
+    def rows_of(first):
+        return pl.ds(pl.multiple_of(first + 64 * side, 64), 64)
+
+    for layer, into in enumerate((w_one, w_two)):
+        for step in range(7):
+            group = [[taps[x, zl, layer * 7 + step] for zl in range(4)] for x in range(4)]
+            for h in range(2):
+                for p, plane in enumerate(planes(group, h)):
+                    tap = 4 * step + 2 * h + p
+                    if tap < 27:
+                        a, b, e = tap // 9, tap // 3 % 3, tap % 3
+                        into[b, rows_of(e * 128), a * 128 : (a + 1) * 128] = plane
+    for first, count, into in ((0, ROWS, act), (ROWS, COTS, cot)):
+        for r in range(count):
+            group = [[rows[zl * 4 + x, first + r] for zl in range(4)] for x in range(4)]
+            for h in range(2):
+                for p, plane in enumerate(planes(group, h)):
+                    into[rows_of((2 * h + p) * 128), r * 128 : (r + 1) * 128] = plane
+
+
+def place_mine(place, mine, taps, act, cot, w_one, w_two):
+    place_half(place[0], mine, taps, act, cot, w_one, w_two)
+
+
 def work(
-    place, mine, other, mine_taps, other_taps, out_tiles, grads,
-    act, hid, err, cot, w_one, w_two, w_back, pre, shifted, total, tiles, sent,
+    place, far, other_taps, act_in, cot_in, one_in, two_in,
+    out_tiles, grads, act, cot, w_one, w_two,
+    hid, err, w_back, pre, shifted, total, tiles, sent,
 ):
     core, chip = place[0], place[1]
-
-    even_core = lax.broadcast(core, (16, 2, 8, 128)) == 0
-
-    def load(one, two):
-        one = one.astype(F32).reshape(16, 2, 8, 128)
-        two = two.astype(F32).reshape(16, 2, 8, 128)
-        return jnp.where(even_core, one, two), jnp.where(even_core, two, one)
-
-    def filters(source, step):
-        return jnp.stack([source[x, zl, step] for zl in range(4) for x in range(4)])
-
-    def planes(one, two, h):
-        merged = merge(one[:, h], two[:, h])
-        return [plane.reshape(128, 128) for plane in merged]
-
-    for r in range(ROWS):
-        one, two = load(mine[:, r], other[:, r])
-        for h in range(2):
-            for p, plane in enumerate(planes(one, two, h)):
-                z = 2 * h + p
-                act[z * 128 : (z + 1) * 128, r * 128 : (r + 1) * 128] = plane.astype(BF16)
-    for layer in range(2):
-        for step in range(7):
-            at = layer * 7 + step
-            one, two = load(filters(mine_taps, at), filters(other_taps, at))
-            for h in range(2):
-                for p, plane in enumerate(planes(one, two, h)):
-                    tap = 4 * step + 2 * h + p
-                    if tap >= 27:
-                        continue
-                    a, b, e = tap // 9, tap // 3 % 3, tap % 3
-                    into = w_two if layer else w_one
-                    into[b, e * 128 : (e + 1) * 128, a * 128 : (a + 1) * 128] = plane.astype(BF16)
-                    if layer:
-                        a, b, e = 2 - a, 2 - b, 2 - e
-                        w_back[b, e * 128 : (e + 1) * 128, a * 128 : (a + 1) * 128] = plane.T.astype(BF16)
-    for r in range(COTS):
-        one, two = load(mine[:, ROWS + r], other[:, ROWS + r])
-        for h in range(2):
-            for p, plane in enumerate(planes(one, two, h)):
-                z = 2 * h + p
-                cot[z * 128 : (z + 1) * 128, r * 128 : (r + 1) * 128] = plane
+    place_half(1 - core, far, other_taps, act, cot, w_one, w_two)
+    for a in range(3):
+        for b in range(3):
+            for e in range(3):
+                block = w_two[b, e * 128 : (e + 1) * 128, a * 128 : (a + 1) * 128]
+                w_back[2 - b, (2 - e) * 128 : (3 - e) * 128, (2 - a) * 128 : (3 - a) * 128] = block.T
 
     for z in range(4):
         for r, value in enumerate(conv_plane(w_one, act, z, 6, 0)):
@@ -157,20 +150,19 @@
         values = conv_plane(w_two, hid, z, 4, 0)
         for r, value in enumerate(values):
             at = (slice(z * 128, (z + 1) * 128), slice(r * 128, (r + 1) * 128))
-            error = cot[at] * jnp.where(value > 0, 1.0, SLOPE)
+            error = cot[at].astype(F32) * jnp.where(value > 0, 1.0, SLOPE)
             err[at] = error.astype(BF16)
             if r in (1, 2):
                 put_errors(shifted, error, core, z, r - 1)
         own = jnp.where(core == 0, values[1], values[2])
-        held[z % 2] = jnp.where(own > 0, own, SLOPE * own).reshape(16, 8, 128)
+        held[z % 2] = jnp.where(own > 0, own, SLOPE * own).reshape(2, 4, 2, 8, 128)
         if z % 2:
-            low = low_half((16, 8, 128))
-            rows = slice((z // 2) * 8, (z // 2) * 8 + 8)
-            for c, tile in enumerate((
-                jnp.where(low, held[0], swap_halves(held[1])),
-                jnp.where(low, swap_halves(held[0]), held[1]),
-            )):
-                tiles[:, c, rows] = tile.astype(BF16)
+            half = slice((z // 2) * 8, (z // 2) * 8 + 8)
+            for odd, tile in enumerate(merge(held[0], held[1])):
+                for c in range(2):
+                    for x in range(4):
+                        for pair in range(2):
+                            tiles[(2 * pair + odd) * 4 + x, c, half] = tile[c, x, pair].astype(BF16)
     send = pltpu.make_async_copy(tiles, out_tiles, sent)
     send.start()
 
@@ -189,23 +181,30 @@
     send.wait()
 
 
-def compute(place, *arrays):
-    vmem = pl.BlockSpec(memory_space=pltpu.VMEM)
-    return pl.pallas_call(
+def compute(place, mine, far, mine_taps, other_taps):
+    smem = pl.BlockSpec(memory_space=pltpu.SMEM)
+    halves = (
+        jax.ShapeDtypeStruct((512, ROWS * 128), BF16),
+        jax.ShapeDtypeStruct((512, COTS * 128), BF16),
+        jax.ShapeDtypeStruct((3, 384, 384), BF16),
+        jax.ShapeDtypeStruct((3, 384, 384), BF16),
+    )
+    half = on_chip(
+        place_mine, halves, [smem, VMEM, VMEM], place, mine, mine_taps, out_specs=(VMEM,) * 4, name="place_mine"
+    )
+    tiles, grads, *_ = on_chip(
         work,
-        out_shape=(
+        (
             jax.ShapeDtypeStruct((16, 2, 16, 128), BF16),
             jax.ShapeDtypeStruct((4, 4, 14, 16, 128), BF16),
+            *halves,
         ),
-        in_specs=[pl.BlockSpec(memory_space=pltpu.SMEM), vmem, vmem, vmem, vmem],
-        out_specs=(pl.BlockSpec(memory_space=pltpu.HBM), vmem),
+        [smem] + [VMEM] * 6, place, far, other_taps, *half,
+        out_specs=(HBM,) + (VMEM,) * 5,
+        input_output_aliases={3: 2, 4: 3, 5: 4, 6: 5},
         scratch_shapes=[
-            pltpu.VMEM((512, 1024), BF16),
             pltpu.VMEM((512, 768), BF16),
             pltpu.VMEM((512, 512), BF16),
-            pltpu.VMEM((512, 512), F32),
-            pltpu.VMEM((3, 384, 384), BF16),
-            pltpu.VMEM((3, 384, 384), BF16),
             pltpu.VMEM((3, 384, 384), BF16),
             pltpu.VMEM((512, 256), F32),
             pltpu.VMEM((192, 1024), BF16),
@@ -213,16 +212,17 @@
             pltpu.VMEM((16, 2, 16, 128), BF16),
             pltpu.SemaphoreType.DMA,
         ],
-        compiler_params=pltpu.CompilerParams(vmem_limit_bytes=48 * 1024 * 1024),
         cost_estimate=pl.CostEstimate(flops=6_300_000_000, bytes_accessed=6_000_000, transcendentals=0),
         name="convolutions",
-    )(place, *arrays)
+    )
+    return tiles, grads
 
 
 def pack_taps(one, two, out, near, sems):
     copies = [pltpu.make_async_copy(taps, near.at[n], sems.at[n]) for n, taps in enumerate((one, two))]
     for copy in copies:
         copy.start()
+    order = channel_order()
     for layer, copy in enumerate(copies):
         copy.wait()
         for step in range(7):
@@ -230,11 +230,12 @@
             if len(parts) == 3:
                 parts.append(jnp.zeros((4, 128), F32))
             tile = jnp.concatenate(parts, 0).astype(BF16)
+            tile = jnp.dot(tile, order, preferred_element_type=F32).astype(BF16)
             for zl in range(4):
                 out[zl, layer * 7 + step] = tile
 
 
-def pack_rows(volume, cotangent, after, out):
+def pack_rows(volume, cotangent, out, near, sems):
     for source, start, halo, count in ((volume, 0, 3, ROWS), (cotangent, ROWS, 1, COTS)):
         planes = [source[ch, z].astype(F32) for z in range(4) for ch in range(4)]
         rows = jnp.swapaxes(jnp.stack(planes), 0, 1).astype(BF16)
@@ -242,26 +243,38 @@
             for r in range(count):
                 row = 2 * chip + r - halo
                 if 0 <= row < 32:
-                    out[chip, start + r] = rows[row]
+                    near[chip, start + r] = rows[row]
                 else:
-                    out[chip, start + r] = jnp.zeros((16, 128), BF16)
+                    near[chip, start + r] = jnp.zeros((16, 128), BF16)
+    copies = [pltpu.make_async_copy(near.at[chip], out.at[chip], sems.at[chip]) for chip in range(16)]
+    for copy in copies:
+        copy.start()
+    for copy in copies:
+        copy.wait()
+
+
+def hold(packed, after, out):
+    pass
 
 
 def sum_pieces(pieces, tiles, total, kept):
-    total[...] = pieces[...].astype(F32).sum(0).astype(BF16)
+    found = pieces[...].astype(F32).sum(0).astype(BF16)
+    total[...] = lax.dot_general(
+        found, channel_order(), (((1,), (1,)), ((), ())), preferred_element_type=F32
+    ).astype(BF16)
 
 
 VMEM = pl.BlockSpec(memory_space=pltpu.VMEM)
 HBM = pl.BlockSpec(memory_space=pltpu.HBM)
 
 
-def on_chip(kernel, shapes, specs, *arrays, out_specs=VMEM, **options):
+def on_chip(kernel, shapes, specs, *arrays, out_specs=VMEM, room=24, **options):
     return pl.pallas_call(
         kernel,
         out_shape=shapes,
         in_specs=specs,
         out_specs=out_specs,
-        compiler_params=pltpu.CompilerParams(vmem_limit_bytes=24 * 1024 * 1024),
+        compiler_params=pltpu.CompilerParams(vmem_limit_bytes=room * 1024 * 1024),
         **options,
     )(*arrays)
 
@@ -281,12 +294,19 @@
         pack_taps, jax.ShapeDtypeStruct((4, 14, 16, 128), BF16), [HBM, HBM],
         own_taps(weight_one), own_taps(weight_two),
         scratch_shapes=[pltpu.VMEM((2, 27, 4, 128), BF16), pltpu.SemaphoreType.DMA((2,))],
-        name="pack_taps",
+        room=60, name="pack_taps",
     )
     line = exchange(taps, "zl")
     packed = on_chip(
-        pack_rows, jax.ShapeDtypeStruct((16, ROWS + COTS, 16, 128), BF16), [VMEM, VMEM, HBM],
-        activations[0], grad_out[0], line, name="pack_rows",
+        pack_rows, jax.ShapeDtypeStruct((16, ROWS + COTS, 16, 128), BF16), [VMEM, VMEM],
+        activations[0], grad_out[0], out_specs=HBM, scratch_shapes=[
+            pltpu.VMEM((16, ROWS + COTS, 16, 128), BF16), pltpu.SemaphoreType.DMA((16,)),
+        ],
+        name="pack_rows",
+    )
+    packed = on_chip(
+        hold, jax.ShapeDtypeStruct(packed.shape, BF16), [HBM, HBM], packed, line,
+        out_specs=HBM, input_output_aliases={0: 0}, name="hold",
     )
     mine = exchange(packed, CHIPS)
     mine_taps = lax.all_gather(line[None], "x", axis=0, tiled=True)

time: 129 us -> 128 us (level)
  blocking collectives: 95.5 us -> 81.8 us
  starting transfers between devices: 17.4 us -> 23.4 us
  waiting for transfers between devices: 1.94 us -> 7.82 us
  Pallas kernels: 9.97 us -> 11.9 us
  local copies, waits for them, and re-layouts: 2.92 us -> 1.44 us
    all_to_all x3 -> x2, blocking collectives: 65 us -> 51.3 us  [exchange(): return lax.all_to_all(array, axis, split_axis=0, concat_axis=0, tiled=True)]
    pallas_call x3 -> x6, Pallas kernels: 1.12 us -> 11.9 us  [on_chip(): pl.pallas_call(kernel, out_shape=shapes, in_specs=specs, out_specs=out_sp...]
    pallas_call x1 -> x0, Pallas kernels: 8.86 us -> none  [compute(): pl.pallas_call(work, out_shape=(jax.ShapeDtypeStruct((16, 2, 16, 128), BF...]
    all_to_all x2 -> x3, waiting for transfers between devices: 0.01 us -> 7.05 us  [exchange(): return lax.all_to_all(array, axis, split_axis=0, concat_axis=0, tiled=True)]
    all_to_all x2 -> x3, starting transfers between devices: 13.1 us -> 19 us  [exchange(): return lax.all_to_all(array, axis, split_axis=0, concat_axis=0, tiled=True)]
    unnamed x9 -> x5, local copies, waits for them, and re-layouts: 2.16 us -> 0.68 us
  transfers between devices with their start and end apart: 4 -> 5, of which waited for: 1 -> 2; matrix products, arithmetic and copies ran while one was open for 1% -> 1% of each run, Pallas kernels for 0% -> 2%
where the time goes in v3:
time: 128 us; the launch traced here: 127 us
  blocking collectives  81.8 us (64%)
  starting transfers between devices  23.4 us (18%)
  Pallas kernels  11.9 us (9%)
  waiting for transfers between devices  7.82 us (6%)
  local copies, waits for them, and re-layouts  1.44 us (1%)
    all_to_all x2, blocking collectives, exchange(): return lax.all_to_all(array, axis, split_axis=0, concat_axis=0, tiled=True)  51.3 us
    all_to_all x3, starting transfers between devices, exchange(): return lax.all_to_all(array, axis, split_axis=0, concat_axis=0, tiled=True)  19 us
    all_gather x1, blocking collectives, on_device(): mine_taps = lax.all_gather(line[None], 'x', axis=0, tiled=True)  18.6 us
    pallas_call x6, Pallas kernels, on_chip(): pl.pallas_call(kernel, out_shape=shapes, in_specs=specs, out_specs=out_sp...  11.9 us
    all_gather x1, blocking collectives, on_device(): every = lax.all_gather(piece[None], 'y', axis=0, tiled=True)  11.9 us
    all_to_all x3, waiting for transfers between devices, exchange(): return lax.all_to_all(array, axis, split_axis=0, concat_axis=0, tiled=True)  7.05 us
  transfers between devices with their start and end apart: 5, of which 2 were waited for; matrix products, arithmetic and copies ran while one was open for 1% of the time, Pallas kernels for 2%

profile of v3, /device:TPU:2, one launch (start us, length us, event | category | flops | bytes accessed | tf_op | source)
XLA Modules:
  0.0 127.3 jit_solution(4422812489468669009)
XLA Ops:
  0.6 1.8 %pack_taps.1 = bf16[4,14,16,128]{3,2,1,0:T(8,128)(2,1)} custom-call(bf16[27,4,128]{2,1,0:T(4,128)(2,1)} %bitcast.44, bf16[27,4,128]{2,1,0:T(4,128)(2,1)} %bitcast.45), custom_call_target="tpu_custom_call" | custom-call | tf_op jit(solution)/shard_map/pack_taps/pallas_call | solution.py:272
  2.4 0.0 copy-start
  2.5 0.0 copy-start.1
  2.5 6.0 %all-to-all-start = ((bf16[4,14,16,128]{3,2,1,0:T(8,128)(2,1)}), bf16[4,14,16,128]{3,2,1,0:T(8,128)(2,1)S(1)}, u32[]{:S(2)}, u32[]{:S(2)}) async-start(bf16[4,14,16,128]{3,2,1,0:T(8,128)(2,1)} %pack_taps.1), calls=%async_computation | async-start | bytes 458752 | tf_op jit(solution)/shard_map/all_to_all | solution.py:287
  8.5 0.0 copy-done
  8.5 0.0 copy-done.1
  8.5 1.2 pack_rows.1.packed
  9.7 7.0 %all-to-all-done.after = bf16[4,14,16,128]{3,2,1,0:T(8,128)(2,1)S(1)} async-done(((bf16[4,14,16,128]{3,2,1,0:T(8,128)(2,1)}), bf16[4,14,16,128]{3,2,1,0:T(8,128)(2,1)S(1)}, u32[]{:S(2)}, u32[]{:S(2)}) %all-to-all-start) | async-done | bytes 229408 | tf_op jit(solution)/shard_map/all_to_all | solution.py:287
  16.7 5.7 %all-to-all-start.1 = ((bf16[16,12,16,128]{3,2,1,0:T(8,128)(2,1)}), bf16[16,12,16,128]{3,2,1,0:T(8,128)(2,1)S(1)}, u32[]{:S(2)}, u32[]{:S(2)}) async-start(bf16[16,12,16,128]{3,2,1,0:T(8,128)(2,1)} %hold.1), calls=%async_computation.1 | async-start | bytes 1572864 | tf_op jit(solution)/shard_map/all_to_all | solution.py:287
  22.4 18.6 %all-gather = bf16[16,14,16,128]{3,2,1,0:T(8,128)(2,1)S(1)} all-gather(bf16[4,14,16,128]{3,2,1,0:T(8,128)(2,1)S(1)} %all-to-all-done.after), channel_id=2, replica_groups=mesh['zl'=4,'x'=4,'c'=2,'zh'=4,'y'=4] {'x'}, dimensions={0}, use_global_device_ids=true | all-gather | bytes 1146880 | tf_op jit(solution)/shard_map/all_gather | solution.py:312
  41.0 1.9 %collective-permute-start.1 = (bf16[4,4,14,16,128]{4,3,2,1,0:T(8,128)(2,1)S(1)}, bf16[4,4,14,16,128]{4,3,2,1,0:T(8,128)(2,1)S(1)}, u32[]{:S(2)}, u32[]{:S(2)}) collective-permute-start(bf16[4,4,14,16,128]{4,3,2,1,0:T(8,128)(2,1)S(1)} %bitcast.31), channel_id=1, source_target_pairs={{0,16},{16,0},{1,17},{17,1},{2,18},{18,2},{3,19},{19,3},{4,20},{20... | collective-permute-start | bytes 2752520 | tf_op jit(solution)/shard_map/ppermute | solution.py:314
  43.0 0.0 all-to-all-done.1.mine
  43.0 2.4 %collective-permute-start = (bf16[16,12,16,128]{3,2,1,0:T(8,128)(2,1)S(1)}, bf16[16,12,16,128]{3,2,1,0:T(8,128)(2,1)S(1)}, u32[]{:S(2)}, u32[]{:S(2)}) collective-permute-start(bf16[16,12,16,128]{3,2,1,0:T(8,128)(2,1)S(1)} %all-to-all-done.1.mine), channel_id=1, source_target_pairs={{0,16},{16,0},{1,17},{17,1},{2,18},{18,2},{3,19},{19,3},{4,20},{20... | collective-permute-start | bytes 2359304 | tf_op jit(solution)/shard_map/ppermute | solution.py:314
  45.4 0.1 pad_add_fusion.place
  45.5 1.0 place_mine.1
  46.5 0.0 collective-permute-done.1.other_taps
  46.5 0.8 collective-permute-done.far
  47.3 7.7 %convolutions.1 = (bf16[16,2,16,128]{3,2,1,0:T(8,128)(2,1)}, bf16[4,4,14,16,128]{4,3,2,1,0:T(8,128)(2,1)S(1)}, bf16[512,1024]{1,0:T(8,128)(2,1)S(1)}, bf16[512,5...) custom-call(s32[2]{0:T(128)S(1)} %pad_add_fusion.place, ...), custom_call_target="tpu_custom_call", output_to_operand_aliasing={{2}: (3, {}), {3}: (4, {}), {4}: (5, {}), {5}: (6, {})} | custom-call | flops 6300000256 | bytes 6000000 | tf_op jit(solution)/shard_map/convolutions/pallas_call | solution.py:272
  55.0 21.0 %all_to_all.25 = bf16[16,14,16,128]{3,2,1,0:T(8,128)(2,1)S(1)} all-to-all(bf16[16,14,16,128]{3,2,1,0:T(8,128)(2,1)S(1)} %bitcast.33), channel_id=1, replica_groups=mesh['zl'=4,'x'=4,'c'=2,'zh'=4,'y'=4] {'x','y'}, dimensions={0} | all-to-all | bytes 1835008 | tf_op jit(solution)/shard_map/all_to_all | solution.py:287
  76.1 0.1 reduce_sum.12
  76.3 30.3 %all_to_all.26.pieces = bf16[16,56,128]{2,1,0:T(8,128)(2,1)S(1)} all-to-all(bf16[16,56,128]{2,1,0:T(8,128)(2,1)S(1)} %bitcast.36), channel_id=1, replica_groups=mesh['zl'=4,'x'=4,'c'=2,'zh'=4,'y'=4] {'zh','zl'}, dimensions={0} | all-to-all | bytes 458752 | tf_op jit(solution)/shard_map/all_to_all | solution.py:287
  106.5 0.2 sum_pieces.1
  106.7 7.3 %all-to-all-start.4 = ((bf16[32,16,128]{2,1,0:T(8,128)(2,1)}), bf16[32,16,128]{2,1,0:T(8,128)(2,1)S(1)}, u32[]{:S(2)}, u32[]{:S(2)}) async-start(bf16[32,16,128]{2,1,0:T(8,128)(2,1)} %bitcast.14), calls=%async_computation.4 | async-start | bytes 262144 | tf_op jit(solution)/shard_map/all_to_all | solution.py:287
  114.0 11.9 %all-gather.1 = bf16[224,128]{1,0:T(8,128)(2,1)S(1)} all-gather(bf16[56,128]{1,0:T(8,128)(2,1)S(1)} %get-tuple-element.18), channel_id=3, replica_groups=mesh['zl'=4,'x'=4,'c'=2,'zh'=4,'y'=4] {'y'}, dimensions={0}, use_global_device_ids=true | all-gather | bytes 71680 | tf_op jit(solution)/shard_map/all_gather | solution.py:332
  125.9 0.6 fusion
  126.6 0.0 all-to-all-done.4
  126.6 0.7 copy.23
  (6 shorter events, 0.1 us)
Async XLA Ops:
  2.4 6.1 %copy-start = (bf16[1,4,4,32,128]{4,3,2,1,0:T(8,128)(2,1)S(1)}, bf16[1,4,4,32,128]{4,3,2,1,0:T(8,128)(2,1)}, u32[]{:S(2)}) copy-start(bf16[1,4,4,32,128]{4,3,2,1,0:T(8,128)(2,1)} %param.4) | copy-start | bytes 393220
  2.5 6.1 %copy-start.1 = (bf16[1,4,4,32,128]{4,3,2,1,0:T(8,128)(2,1)S(1)}, bf16[1,4,4,32,128]{4,3,2,1,0:T(8,128)(2,1)}, u32[]{:S(2)}) copy-start(bf16[1,4,4,32,128]{4,3,2,1,0:T(8,128)(2,1)} %param.7) | copy-start | bytes 393220
  2.5 14.3 %all-to-all-start = ((bf16[4,14,16,128]{3,2,1,0:T(8,128)(2,1)}), bf16[4,14,16,128]{3,2,1,0:T(8,128)(2,1)S(1)}, u32[]{:S(2)}, u32[]{:S(2)}) async-start(bf16[4,14,16,128]{3,2,1,0:T(8,128)(2,1)} %pack_taps.1), calls=%async_computation | async-start | bytes 458752 | tf_op jit(solution)/shard_map/all_to_all | solution.py:287
  16.7 26.2 %all-to-all-start.1 = ((bf16[16,12,16,128]{3,2,1,0:T(8,128)(2,1)}), bf16[16,12,16,128]{3,2,1,0:T(8,128)(2,1)S(1)}, u32[]{:S(2)}, u32[]{:S(2)}) async-start(bf16[16,12,16,128]{3,2,1,0:T(8,128)(2,1)} %hold.1), calls=%async_computation.1 | async-start | bytes 1572864 | tf_op jit(solution)/shard_map/all_to_all | solution.py:287
  41.0 5.5 %collective-permute-start.1 = (bf16[4,4,14,16,128]{4,3,2,1,0:T(8,128)(2,1)S(1)}, bf16[4,4,14,16,128]{4,3,2,1,0:T(8,128)(2,1)S(1)}, u32[]{:S(2)}, u32[]{:S(2)}) collective-permute-start(bf16[4,4,14,16,128]{4,3,2,1,0:T(8,128)(2,1)S(1)} %bitcast.31), channel_id=1, source_target_pairs={{0,16},{16,0},{1,17},{17,1},{2,18},{18,2},{3,19},{19,3},{4,20},{20... | collective-permute-start | bytes 2752520 | tf_op jit(solution)/shard_map/ppermute | solution.py:314
  43.0 4.3 %collective-permute-start = (bf16[16,12,16,128]{3,2,1,0:T(8,128)(2,1)S(1)}, bf16[16,12,16,128]{3,2,1,0:T(8,128)(2,1)S(1)}, u32[]{:S(2)}, u32[]{:S(2)}) collective-permute-start(bf16[16,12,16,128]{3,2,1,0:T(8,128)(2,1)S(1)} %all-to-all-done.1.mine), channel_id=1, source_target_pairs={{0,16},{16,0},{1,17},{17,1},{2,18},{18,2},{3,19},{19,3},{4,20},{20... | collective-permute-start | bytes 2359304 | tf_op jit(solution)/shard_map/ppermute | solution.py:314
  106.7 19.9 %all-to-all-start.4 = ((bf16[32,16,128]{2,1,0:T(8,128)(2,1)}), bf16[32,16,128]{2,1,0:T(8,128)(2,1)S(1)}, u32[]{:S(2)}, u32[]{:S(2)}) async-start(bf16[32,16,128]{2,1,0:T(8,128)(2,1)} %bitcast.14), calls=%async_computation.4 | async-start | bytes 262144 | tf_op jit(solution)/shard_map/all_to_all | solution.py:287

commit v4 on v3

--- a/solution.py
+++ b/solution.py
@@ -126,7 +126,7 @@
 def work(
     place, far, other_taps, act_in, cot_in, one_in, two_in,
     out_tiles, grads, act, cot, w_one, w_two,
-    hid, err, w_back, pre, shifted, total, tiles, sent,
+    hid, err, w_back, pre, shifted, total,
 ):
     core, chip = place[0], place[1]
     place_half(1 - core, far, other_taps, act, cot, w_one, w_two)
@@ -162,9 +162,7 @@
                 for c in range(2):
                     for x in range(4):
                         for pair in range(2):
-                            tiles[(2 * pair + odd) * 4 + x, c, half] = tile[c, x, pair].astype(BF16)
-    send = pltpu.make_async_copy(tiles, out_tiles, sent)
-    send.start()
+                            out_tiles[(2 * pair + odd) * 4 + x, c, half] = tile[c, x, pair].astype(BF16)
 
     for x in range(4):
         for g in range(2):
@@ -178,7 +176,6 @@
             )
             put_errors(shifted, value * slope, core, z, r)
     tap_grad(shifted, act, 2, total, grads, 0)
-    send.wait()
 
 
 def compute(place, mine, far, mine_taps, other_taps):
@@ -200,7 +197,7 @@
             *halves,
         ),
         [smem] + [VMEM] * 6, place, far, other_taps, *half,
-        out_specs=(HBM,) + (VMEM,) * 5,
+        out_specs=(VMEM,) * 6,
         input_output_aliases={3: 2, 4: 3, 5: 4, 6: 5},
         scratch_shapes=[
             pltpu.VMEM((512, 768), BF16),
@@ -209,8 +206,6 @@
             pltpu.VMEM((512, 256), F32),
             pltpu.VMEM((192, 1024), BF16),
             pltpu.VMEM((192, 384), F32),
-            pltpu.VMEM((16, 2, 16, 128), BF16),
-            pltpu.SemaphoreType.DMA,
         ],
         cost_estimate=pl.CostEstimate(flops=6_300_000_000, bytes_accessed=6_000_000, transcendentals=0),
         name="convolutions",
@@ -225,14 +220,11 @@
     order = channel_order()
     for layer, copy in enumerate(copies):
         copy.wait()
-        for step in range(7):
-            parts = [near[layer, 4 * step + t].astype(F32) for t in range(min(4, 27 - 4 * step))]
-            if len(parts) == 3:
-                parts.append(jnp.zeros((4, 128), F32))
-            tile = jnp.concatenate(parts, 0).astype(BF16)
-            tile = jnp.dot(tile, order, preferred_element_type=F32).astype(BF16)
-            for zl in range(4):
-                out[zl, layer * 7 + step] = tile
+        parts = [near[layer, t].astype(F32) for t in range(27)] + [jnp.zeros((4, 128), F32)]
+        taps = jnp.concatenate(parts, 0).astype(BF16)
+        taps = jnp.dot(taps, order, preferred_element_type=F32).astype(BF16)
+        for zl in range(4):
+            out[zl, layer * 7 : layer * 7 + 7] = taps.reshape(7, 16, 128)
 
 
 def pack_rows(volume, cotangent, out, near, sems):
@@ -257,11 +249,52 @@
     pass
 
 
-def sum_pieces(pieces, tiles, total, kept):
+def sum_ring(parts, after, out):
+    total = parts[0].astype(F32)
+    for n in range(1, 16):
+        total = total + parts[n].astype(F32)
+    total = total.reshape(7, 2, 2, 8, 128)
+    for h in range(2):
+        for p, piece in enumerate(merge(total[:, 0, h], total[:, 1, h])):
+            piece = piece.reshape(56, 128).astype(BF16)
+            for zh in range(4):
+                out[zh * 4 + 2 * h + p] = piece
+
+
+def sum_pieces(pieces, total):
     found = pieces[...].astype(F32).sum(0).astype(BF16)
-    total[...] = lax.dot_general(
+    found = lax.dot_general(
         found, channel_order(), (((1,), (1,)), ((), ())), preferred_element_type=F32
     ).astype(BF16)
+    for y in range(4):
+        total[y] = found
+
+
+def pick_line(place, line, after, out):
+    for zl in range(4):
+        out[zl] = line[zl, place[1] // 4]
+
+
+def pick_ring(place, ring, out):
+    for x in range(4):
+        for zl in range(4):
+            out[x, zl] = ring[x, zl, place[1] % 4, 1 - place[0]]
+
+
+def join_rows(place, ring, other, out, near, sent):
+    core, tiles = place[0], []
+    for zl in range(4):
+        for x in range(4):
+            mine = ring[x, zl, place[1] % 4, core].astype(F32)
+            came = other[x, zl].astype(F32)
+            tiles += [jnp.where(core == 0, mine, came), jnp.where(core == 0, came, mine)]
+    rows = jnp.swapaxes(jnp.stack(tiles), 0, 1).astype(BF16)
+    for z in range(4):
+        for ch in range(4):
+            near[ch, z] = rows[z * 4 + ch]
+    copy = pltpu.make_async_copy(near, out, sent)
+    copy.start()
+    copy.wait()
 
 
 VMEM = pl.BlockSpec(memory_space=pltpu.VMEM)
@@ -316,26 +349,33 @@
     tiles, grads = compute(place, mine, other, mine_taps, other_taps)
 
     parts = exchange(grads.reshape(16, 14, 16, 128), ("x", "y"))
-    summed = parts.astype(F32).sum(0).astype(BF16)
-    pieces = jnp.transpose(summed.reshape(14, 4, 4, 128), (1, 0, 2, 3)).reshape(1, 4, 56, 128)
-    spread = jnp.broadcast_to(pieces, (4, 4, 56, 128)).reshape(16, 56, 128)
+    out_line = lax.all_gather(tiles.reshape(1, 4, 4, 2, 16, 128), "zl", axis=0, tiled=True)
+    spread = on_chip(
+        sum_ring, jax.ShapeDtypeStruct((16, 56, 128), BF16), [VMEM, HBM], parts, out_line, name="sum_ring"
+    )
     depth = exchange(spread, ("zh", "zl"))
-
-    piece, tiles = on_chip(
-        sum_pieces,
-        (jax.ShapeDtypeStruct((56, 128), BF16), jax.ShapeDtypeStruct(tiles.shape, BF16)),
-        [VMEM, HBM], depth, tiles,
-        out_specs=(VMEM, HBM),
-        input_output_aliases={1: 1},
-        name="sum_pieces",
-    )
-    every = lax.all_gather(piece[None], "y", axis=0, tiled=True)
+    piece = on_chip(sum_pieces, jax.ShapeDtypeStruct((4, 56, 128), BF16), [VMEM], depth, name="sum_pieces")
+    every = exchange(piece, "y")
     found = jnp.transpose(every.reshape(4, 2, 7, 4, 128), (1, 0, 2, 3, 4)).reshape(2, 28, 4, 128)
     found = jnp.transpose(found[:, :27].astype(F32), (0, 1, 3, 2)).reshape(2, 3, 3, 3, 128, 4)
 
-    rows = exchange(tiles.reshape(32, 16, 128), FILT)
-    result = jnp.transpose(rows.reshape(32, 4, 4, 128), (2, 1, 0, 3))[None]
-    return (result, found[0], found[1])
+    smem = pl.BlockSpec(memory_space=pltpu.SMEM)
+    out_line = on_chip(
+        pick_line, jax.ShapeDtypeStruct((4, 4, 2, 16, 128), BF16), [smem, VMEM, HBM],
+        place, out_line, spread, name="pick_line",
+    )
+    out_ring = lax.all_gather(out_line[None], "x", axis=0, tiled=True)
+    sent = on_chip(
+        pick_ring, jax.ShapeDtypeStruct((4, 4, 16, 128), BF16), [smem, VMEM], place, out_ring, name="pick_ring"
+    )
+    result = on_chip(
+        join_rows, jax.ShapeDtypeStruct((4, 4, 32, 128), BF16), [smem, VMEM, VMEM],
+        place, out_ring, lax.ppermute(sent, "c", swap),
+        out_specs=HBM,
+        scratch_shapes=[pltpu.VMEM((4, 4, 32, 128), BF16), pltpu.SemaphoreType.DMA],
+        name="join_rows",
+    )
+    return (result[None], found[0], found[1])
 
 
 def solution(mesh):

time: 128 us -> 122 us (0.953)
  the two profiles are of different devices: /device:TPU:2 before, /device:TPU:1 now
where the time goes in v4:
time: 122 us
  starting transfers between devices  52 us (43%)
  blocking collectives  43.2 us (35%)
  Pallas kernels  16.5 us (14%)
  waiting for transfers between devices  8.46 us (7%)
    all_to_all x5, starting transfers between devices, exchange(): return lax.all_to_all(array, axis, split_axis=0, concat_axis=0, tiled=True)  36.4 us
    all_gather x1, blocking collectives, on_device(): mine_taps = lax.all_gather(line[None], 'x', axis=0, tiled=True)  17.7 us
    pallas_call x10, Pallas kernels, on_chip(): pl.pallas_call(kernel, out_shape=shapes, in_specs=specs, out_specs=out_sp...  16.5 us
    all_gather x1, blocking collectives, on_device(): lax.all_gather(tiles.reshape(1, 4, 4, 2, 16, 128), 'zl', axis=0, tiled=True)  15.3 us
    all_gather x1, blocking collectives, on_device(): out_ring = lax.all_gather(out_line[None], 'x', axis=0, tiled=True)  10.2 us
    ppermute x1, starting transfers between devices, on_device(): lax.ppermute(sent, 'c', swap)  7.87 us
    all_to_all x5, waiting for transfers between devices, exchange(): return lax.all_to_all(array, axis, split_axis=0, concat_axis=0, tiled=True)  7.33 us
    ppermute x1, starting transfers between devices, on_device(): lax.ppermute(mine_taps, 'c', swap)  5.86 us
  transfers between devices with their start and end apart: 8, of which 3 were waited for; matrix products, arithmetic and copies ran while one was open for 0% of the time, Pallas kernels for 4%

profile of v4, /device:TPU:1, one launch (start us, length us, event | category | flops | bytes accessed | tf_op | source)
XLA Modules:
  0.0 121.7 jit_solution(3057346146906271694)
XLA Ops:
  0.6 1.8 %pack_taps.1 = bf16[4,14,16,128]{3,2,1,0:T(8,128)(2,1)} custom-call(bf16[27,4,128]{2,1,0:T(4,128)(2,1)} %bitcast.35, bf16[27,4,128]{2,1,0:T(4,128)(2,1)} %bitcast.36), custom_call_target="tpu_custom_call" | custom-call | tf_op jit(solution)/shard_map/pack_taps/pallas_call | solution.py:305
  2.4 0.0 copy-start
  2.4 0.0 copy-start.1
  2.4 6.6 %all-to-all-start = ((bf16[4,14,16,128]{3,2,1,0:T(8,128)(2,1)}), bf16[4,14,16,128]{3,2,1,0:T(8,128)(2,1)S(1)}, u32[]{:S(2)}, u32[]{:S(2)}) async-start(bf16[4,14,16,128]{3,2,1,0:T(8,128)(2,1)} %pack_taps.1), calls=%async_computation | async-start | bytes 458752 | tf_op jit(solution)/shard_map/all_to_all | solution.py:320
  9.0 0.0 copy-done
  9.0 0.0 copy-done.1
  9.0 1.2 pack_rows.1.packed
  10.2 4.2 %all-to-all-done.after = bf16[4,14,16,128]{3,2,1,0:T(8,128)(2,1)S(1)} async-done(((bf16[4,14,16,128]{3,2,1,0:T(8,128)(2,1)}), bf16[4,14,16,128]{3,2,1,0:T(8,128)(2,1)S(1)}, u32[]{:S(2)}, u32[]{:S(2)}) %all-to-all-start) | async-done | bytes 229408 | tf_op jit(solution)/shard_map/all_to_all | solution.py:320
  14.4 7.4 %all-to-all-start.1 = ((bf16[16,12,16,128]{3,2,1,0:T(8,128)(2,1)}), bf16[16,12,16,128]{3,2,1,0:T(8,128)(2,1)S(1)}, u32[]{:S(2)}, u32[]{:S(2)}) async-start(bf16[16,12,16,128]{3,2,1,0:T(8,128)(2,1)} %hold.1), calls=%async_computation.1 | async-start | bytes 1572864 | tf_op jit(solution)/shard_map/all_to_all | solution.py:320
  21.8 17.7 %all-gather = bf16[16,14,16,128]{3,2,1,0:T(8,128)(2,1)S(1)} all-gather(bf16[4,14,16,128]{3,2,1,0:T(8,128)(2,1)S(1)} %all-to-all-done.after), channel_id=2, replica_groups=mesh['zl'=4,'x'=4,'c'=2,'zh'=4,'y'=4] {'x'}, dimensions={0}, use_global_device_ids=true | all-gather | bytes 1146880 | tf_op jit(solution)/shard_map/all_gather | solution.py:345
  39.5 5.9 %collective-permute-start.1 = (bf16[4,4,14,16,128]{4,3,2,1,0:T(8,128)(2,1)S(1)}, bf16[4,4,14,16,128]{4,3,2,1,0:T(8,128)(2,1)S(1)}, u32[]{:S(2)}, u32[]{:S(2)}) collective-permute-start(bf16[4,4,14,16,128]{4,3,2,1,0:T(8,128)(2,1)S(1)} %bitcast.25), channel_id=1, source_target_pairs={{0,16},{16,0},{1,17},{17,1},{2,18},{18,2},{3,19},{19,3},{4,20},{20... | collective-permute-start | bytes 2752520 | tf_op jit(solution)/shard_map/ppermute | solution.py:347
  45.4 0.0 all-to-all-done.1.mine
  45.4 1.9 %collective-permute-start = (bf16[16,12,16,128]{3,2,1,0:T(8,128)(2,1)S(1)}, bf16[16,12,16,128]{3,2,1,0:T(8,128)(2,1)S(1)}, u32[]{:S(2)}, u32[]{:S(2)}) collective-permute-start(bf16[16,12,16,128]{3,2,1,0:T(8,128)(2,1)S(1)} %all-to-all-done.1.mine), channel_id=1, source_target_pairs={{0,16},{16,0},{1,17},{17,1},{2,18},{18,2},{3,19},{19,3},{4,20},{20... | collective-permute-start | bytes 2359304 | tf_op jit(solution)/shard_map/ppermute | solution.py:347
  47.3 0.1 pad_add_fusion.place
  47.4 1.0 place_mine.1
  48.5 0.0 collective-permute-done.1.other_taps
  48.5 1.1 collective-permute-done.far
  49.6 8.5 %convolutions.1 = (bf16[16,2,16,128]{3,2,1,0:T(8,128)(2,1)S(1)}, bf16[4,4,14,16,128]{4,3,2,1,0:T(8,128)(2,1)}, bf16[512,1024]{1,0:T(8,128)(2,1)S(1)}, bf16[512,5...) custom-call(s32[2]{0:T(128)S(1)} %pad_add_fusion.place, ...), custom_call_target="tpu_custom_call", output_to_operand_aliasing={{2}: (3, {}), {3}: (4, {}), {4}: (5, {}), {5}: (6, {})} | custom-call | flops 6300000256 | bytes 6000000 | tf_op jit(solution)/shard_map/convolutions/pallas_call | solution.py:305
  58.1 5.5 %all-to-all-start.2 = ((bf16[16,14,16,128]{3,2,1,0:T(8,128)(2,1)}), bf16[16,14,16,128]{3,2,1,0:T(8,128)(2,1)S(1)}, u32[]{:S(2)}, u32[]{:S(2)}) async-start(bf16[16,14,16,128]{3,2,1,0:T(8,128)(2,1)} %bitcast.10), calls=%async_computation.2 | async-start | bytes 1835008 | tf_op jit(solution)/shard_map/all_to_all | solution.py:320
  63.6 15.3 %all_gather.10.after.line = bf16[4,4,4,2,16,128]{5,4,3,2,1,0:T(8,128)(2,1)S(1)} all-gather(bf16[1,4,4,2,16,128]{5,4,3,2,1,0:T(8,128)(2,1)S(1)} %bitcast.27), channel_id=1, replica_groups=mesh['zl'=4,'x'=4,'c'=2,'zh'=4,'y'=4] {'zl'}, dimensions={0}, use_global_device_ids=true | all-gather | bytes 655360 | tf_op jit(solution)/shard_map/all_gather | solution.py:352
  78.9 0.0 all-to-all-done.2.parts
  78.9 0.8 sum_ring.1.after
  79.7 12.9 %all-to-all-start.3 = ((bf16[16,56,128]{2,1,0:T(8,128)(2,1)}), bf16[16,56,128]{2,1,0:T(8,128)(2,1)S(1)}, u32[]{:S(2)}, u32[]{:S(2)}) async-start(bf16[16,56,128]{2,1,0:T(8,128)(2,1)} %sum_ring.1.after), calls=%async_computation.3 | async-start | bytes 458752 | tf_op jit(solution)/shard_map/all_to_all | solution.py:320
  92.6 0.6 pick_line.1
  93.2 10.2 %all-gather.1 = bf16[16,4,2,16,128]{4,3,2,1,0:T(8,128)(2,1)S(1)} all-gather(bf16[4,4,2,16,128]{4,3,2,1,0:T(8,128)(2,1)S(1)} %pick_line.1), channel_id=3, replica_groups=mesh['zl'=4,'x'=4,'c'=2,'zh'=4,'y'=4] {'x'}, dimensions={0}, use_global_device_ids=true | all-gather | bytes 655360 | tf_op jit(solution)/shard_map/all_gather | solution.py:367
  103.4 0.6 pick_ring.1
  104.0 7.9 %collective-permute-start.2 = (bf16[4,4,16,128]{3,2,1,0:T(8,128)(2,1)S(1)}, bf16[4,4,16,128]{3,2,1,0:T(8,128)(2,1)S(1)}, u32[]{:S(2)}, u32[]{:S(2)}) collective-permute-start(bf16[4,4,16,128]{3,2,1,0:T(8,128)(2,1)S(1)} %pick_ring.1), channel_id=1, source_target_pairs={{0,16},{16,0},{1,17},{17,1},{2,18},{18,2},{3,19},{19,3},{4,20},{20... | collective-permute-start | bytes 196616 | tf_op jit(solution)/shard_map/ppermute | solution.py:373
  111.9 0.0 all-to-all-done.3.pieces
  111.9 0.8 sum_pieces.1
  112.7 4.0 %all-to-all-start.4 = ((bf16[4,56,128]{2,1,0:T(8,128)(2,1)}), bf16[4,56,128]{2,1,0:T(8,128)(2,1)S(1)}, u32[]{:S(2)}, u32[]{:S(2)}) async-start(bf16[4,56,128]{2,1,0:T(8,128)(2,1)} %sum_pieces.1), calls=%async_computation.4 | async-start | bytes 114688 | tf_op jit(solution)/shard_map/all_to_all | solution.py:320
  116.6 0.0 collective-permute-done.2.other
  116.6 1.3 %join_rows.1 = bf16[4,4,32,128]{3,2,1,0:T(8,128)(2,1)} custom-call(s32[2]{0:T(128)S(1)} %pad_add_fusion.place, bf16[4,4,4,2,16,128]{5,4,3,2,1,0:T(8,128)(2,1)S(1)} %bitcast.24, bf16[4,4,16,128]{3,2,1,0:T(8,128)(2,1)S(1)} %collective-permute-done.2.other), custom_call_target="tpu_custom_call" | custom-call | tf_op jit(solution)/shard_map/join_rows/pallas_call | solution.py:305
  117.9 3.1 %all-to-all-done.4 = bf16[4,56,128]{2,1,0:T(8,128)(2,1)S(1)} async-done(((bf16[4,56,128]{2,1,0:T(8,128)(2,1)}), bf16[4,56,128]{2,1,0:T(8,128)(2,1)S(1)}, u32[]{:S(2)}, u32[]{:S(2)}) %all-to-all-start.4) | async-done | bytes 57376 | tf_op jit(solution)/shard_map/all_to_all | solution.py:320
  121.1 0.6 fusion
  (3 shorter events, 0.0 us)
Async XLA Ops:
  2.4 6.6 %copy-start = (bf16[1,4,4,32,128]{4,3,2,1,0:T(8,128)(2,1)S(1)}, bf16[1,4,4,32,128]{4,3,2,1,0:T(8,128)(2,1)}, u32[]{:S(2)}) copy-start(bf16[1,4,4,32,128]{4,3,2,1,0:T(8,128)(2,1)} %param.4) | copy-start | bytes 393220
  2.4 6.6 %copy-start.1 = (bf16[1,4,4,32,128]{4,3,2,1,0:T(8,128)(2,1)S(1)}, bf16[1,4,4,32,128]{4,3,2,1,0:T(8,128)(2,1)}, u32[]{:S(2)}) copy-start(bf16[1,4,4,32,128]{4,3,2,1,0:T(8,128)(2,1)} %param.7) | copy-start | bytes 393220
  2.4 12.0 %all-to-all-start = ((bf16[4,14,16,128]{3,2,1,0:T(8,128)(2,1)}), bf16[4,14,16,128]{3,2,1,0:T(8,128)(2,1)S(1)}, u32[]{:S(2)}, u32[]{:S(2)}) async-start(bf16[4,14,16,128]{3,2,1,0:T(8,128)(2,1)} %pack_taps.1), calls=%async_computation | async-start | bytes 458752 | tf_op jit(solution)/shard_map/all_to_all | solution.py:320
  14.4 31.0 %all-to-all-start.1 = ((bf16[16,12,16,128]{3,2,1,0:T(8,128)(2,1)}), bf16[16,12,16,128]{3,2,1,0:T(8,128)(2,1)S(1)}, u32[]{:S(2)}, u32[]{:S(2)}) async-start(bf16[16,12,16,128]{3,2,1,0:T(8,128)(2,1)} %hold.1), calls=%async_computation.1 | async-start | bytes 1572864 | tf_op jit(solution)/shard_map/all_to_all | solution.py:320
  39.5 8.9 %collective-permute-start.1 = (bf16[4,4,14,16,128]{4,3,2,1,0:T(8,128)(2,1)S(1)}, bf16[4,4,14,16,128]{4,3,2,1,0:T(8,128)(2,1)S(1)}, u32[]{:S(2)}, u32[]{:S(2)}) collective-permute-start(bf16[4,4,14,16,128]{4,3,2,1,0:T(8,128)(2,1)S(1)} %bitcast.25), channel_id=1, source_target_pairs={{0,16},{16,0},{1,17},{17,1},{2,18},{18,2},{3,19},{19,3},{4,20},{20... | collective-permute-start | bytes 2752520 | tf_op jit(solution)/shard_map/ppermute | solution.py:347
  45.4 4.2 %collective-permute-start = (bf16[16,12,16,128]{3,2,1,0:T(8,128)(2,1)S(1)}, bf16[16,12,16,128]{3,2,1,0:T(8,128)(2,1)S(1)}, u32[]{:S(2)}, u32[]{:S(2)}) collective-permute-start(bf16[16,12,16,128]{3,2,1,0:T(8,128)(2,1)S(1)} %all-to-all-done.1.mine), channel_id=1, source_target_pairs={{0,16},{16,0},{1,17},{17,1},{2,18},{18,2},{3,19},{19,3},{4,20},{20... | collective-permute-start | bytes 2359304 | tf_op jit(solution)/shard_map/ppermute | solution.py:347
  58.1 20.7 %all-to-all-start.2 = ((bf16[16,14,16,128]{3,2,1,0:T(8,128)(2,1)}), bf16[16,14,16,128]{3,2,1,0:T(8,128)(2,1)S(1)}, u32[]{:S(2)}, u32[]{:S(2)}) async-start(bf16[16,14,16,128]{3,2,1,0:T(8,128)(2,1)} %bitcast.10), calls=%async_computation.2 | async-start | bytes 1835008 | tf_op jit(solution)/shard_map/all_to_all | solution.py:320
  79.7 32.2 %all-to-all-start.3 = ((bf16[16,56,128]{2,1,0:T(8,128)(2,1)}), bf16[16,56,128]{2,1,0:T(8,128)(2,1)S(1)}, u32[]{:S(2)}, u32[]{:S(2)}) async-start(bf16[16,56,128]{2,1,0:T(8,128)(2,1)} %sum_ring.1.after), calls=%async_computation.3 | async-start | bytes 458752 | tf_op jit(solution)/shard_map/all_to_all | solution.py:320
  104.0 12.6 %collective-permute-start.2 = (bf16[4,4,16,128]{3,2,1,0:T(8,128)(2,1)S(1)}, bf16[4,4,16,128]{3,2,1,0:T(8,128)(2,1)S(1)}, u32[]{:S(2)}, u32[]{:S(2)}) collective-permute-start(bf16[4,4,16,128]{3,2,1,0:T(8,128)(2,1)S(1)} %pick_ring.1), channel_id=1, source_target_pairs={{0,16},{16,0},{1,17},{17,1},{2,18},{18,2},{3,19},{19,3},{4,20},{20... | collective-permute-start | bytes 196616 | tf_op jit(solution)/shard_map/ppermute | solution.py:373
  112.7 8.4 %all-to-all-start.4 = ((bf16[4,56,128]{2,1,0:T(8,128)(2,1)}), bf16[4,56,128]{2,1,0:T(8,128)(2,1)S(1)}, u32[]{:S(2)}, u32[]{:S(2)}) async-start(bf16[4,56,128]{2,1,0:T(8,128)(2,1)} %sum_pieces.1), calls=%async_computation.4 | async-start | bytes 114688 | tf_op jit(solution)/shard_map/all_to_all | solution.py:320

commit v5 on v4

--- a/solution.py
+++ b/solution.py
@@ -126,7 +126,7 @@
 def work(
     place, far, other_taps, act_in, cot_in, one_in, two_in,
     out_tiles, grads, act, cot, w_one, w_two,
-    hid, err, w_back, pre, shifted, total,
+    hid, err, w_back, pre, shifted, total, near, sems,
 ):
     core, chip = place[0], place[1]
     place_half(1 - core, far, other_taps, act, cot, w_one, w_two)
@@ -154,20 +154,22 @@
             err[at] = error.astype(BF16)
             if r in (1, 2):
                 put_errors(shifted, error, core, z, r - 1)
-        own = jnp.where(core == 0, values[1], values[2])
-        held[z % 2] = jnp.where(own > 0, own, SLOPE * own).reshape(2, 4, 2, 8, 128)
-        if z % 2:
-            half = slice((z // 2) * 8, (z // 2) * 8 + 8)
-            for odd, tile in enumerate(merge(held[0], held[1])):
-                for c in range(2):
+        for r in range(2):
+            own = jnp.where(core == 0, values[1 + r][:64], values[1 + r][64:])
+            held[z % 2, r] = jnp.where(own > 0, own, SLOPE * own).reshape(4, 2, 8, 128)
+            if z % 2:
+                half = slice((z // 2) * 8, (z // 2) * 8 + 8)
+                for odd, tile in enumerate(merge(held[0, r], held[1, r])):
                     for x in range(4):
                         for pair in range(2):
-                            out_tiles[(2 * pair + odd) * 4 + x, c, half] = tile[c, x, pair].astype(BF16)
+                            out_tiles[(2 * pair + odd) * 4 + x, r, half] = tile[x, pair].astype(BF16)
 
     for x in range(4):
         for g in range(2):
-            grads[x, 3, g * 7 + 6] = jnp.zeros((16, 128), BF16)
-    tap_grad(shifted, hid, 1, total, grads, 1)
+            near[x, 3, g * 7 + 6] = jnp.zeros((16, 128), BF16)
+    tap_grad(shifted, hid, 1, total, near, 1)
+    second = pltpu.make_async_copy(near.at[:, :, 7:14], grads.at[:, :, 7:14], sems.at[1])
+    second.start()
 
     for z in range(4):
         for r, value in enumerate(conv_plane(w_back, err, z, 2, 0)):
@@ -175,7 +177,11 @@
                 pre[z * 128 : (z + 1) * 128, r * 128 : (r + 1) * 128] > 0, 1.0, SLOPE
             )
             put_errors(shifted, value * slope, core, z, r)
-    tap_grad(shifted, act, 2, total, grads, 0)
+    tap_grad(shifted, act, 2, total, near, 0)
+    first = pltpu.make_async_copy(near.at[:, :, 0:7], grads.at[:, :, 0:7], sems.at[0])
+    first.start()
+    second.wait()
+    first.wait()
 
 
 def compute(place, mine, far, mine_taps, other_taps):
@@ -197,7 +203,7 @@
             *halves,
         ),
         [smem] + [VMEM] * 6, place, far, other_taps, *half,
-        out_specs=(VMEM,) * 6,
+        out_specs=(VMEM, HBM) + (VMEM,) * 4,
         input_output_aliases={3: 2, 4: 3, 5: 4, 6: 5},
         scratch_shapes=[
             pltpu.VMEM((512, 768), BF16),
@@ -206,6 +212,8 @@
             pltpu.VMEM((512, 256), F32),
             pltpu.VMEM((192, 1024), BF16),
             pltpu.VMEM((192, 384), F32),
+            pltpu.VMEM((4, 4, 14, 16, 128), BF16),
+            pltpu.SemaphoreType.DMA((2,)),
         ],
         cost_estimate=pl.CostEstimate(flops=6_300_000_000, bytes_accessed=6_000_000, transcendentals=0),
         name="convolutions",
@@ -261,7 +269,7 @@
                 out[zh * 4 + 2 * h + p] = piece
 
 
-def sum_pieces(pieces, total):
+def sum_pieces(pieces, after, total):
     found = pieces[...].astype(F32).sum(0).astype(BF16)
     found = lax.dot_general(
         found, channel_order(), (((1,), (1,)), ((), ())), preferred_element_type=F32
@@ -275,19 +283,12 @@
         out[zl] = line[zl, place[1] // 4]
 
 
-def pick_ring(place, ring, out):
-    for x in range(4):
-        for zl in range(4):
-            out[x, zl] = ring[x, zl, place[1] % 4, 1 - place[0]]
-
-
-def join_rows(place, ring, other, out, near, sent):
-    core, tiles = place[0], []
+def join_rows(place, ring, after, out, near, sent):
+    tiles = []
     for zl in range(4):
         for x in range(4):
-            mine = ring[x, zl, place[1] % 4, core].astype(F32)
-            came = other[x, zl].astype(F32)
-            tiles += [jnp.where(core == 0, mine, came), jnp.where(core == 0, came, mine)]
+            for r in range(2):
+                tiles.append(ring[x, zl, place[1] % 4, r].astype(F32))
     rows = jnp.swapaxes(jnp.stack(tiles), 0, 1).astype(BF16)
     for z in range(4):
         for ch in range(4):
@@ -354,23 +355,21 @@
         sum_ring, jax.ShapeDtypeStruct((16, 56, 128), BF16), [VMEM, HBM], parts, out_line, name="sum_ring"
     )
     depth = exchange(spread, ("zh", "zl"))
-    piece = on_chip(sum_pieces, jax.ShapeDtypeStruct((4, 56, 128), BF16), [VMEM], depth, name="sum_pieces")
-    every = exchange(piece, "y")
-    found = jnp.transpose(every.reshape(4, 2, 7, 4, 128), (1, 0, 2, 3, 4)).reshape(2, 28, 4, 128)
-    found = jnp.transpose(found[:, :27].astype(F32), (0, 1, 3, 2)).reshape(2, 3, 3, 3, 128, 4)
-
     smem = pl.BlockSpec(memory_space=pltpu.SMEM)
     out_line = on_chip(
         pick_line, jax.ShapeDtypeStruct((4, 4, 2, 16, 128), BF16), [smem, VMEM, HBM],
         place, out_line, spread, name="pick_line",
     )
     out_ring = lax.all_gather(out_line[None], "x", axis=0, tiled=True)
-    sent = on_chip(
-        pick_ring, jax.ShapeDtypeStruct((4, 4, 16, 128), BF16), [smem, VMEM], place, out_ring, name="pick_ring"
-    )
+    piece = on_chip(
+        sum_pieces, jax.ShapeDtypeStruct((4, 56, 128), BF16), [VMEM, HBM], depth, out_ring, name="sum_pieces"
+    )
+    every = exchange(piece, "y")
+    found = jnp.transpose(every.reshape(4, 2, 7, 4, 128), (1, 0, 2, 3, 4)).reshape(2, 28, 4, 128)
+    found = jnp.transpose(found[:, :27].astype(F32), (0, 1, 3, 2)).reshape(2, 3, 3, 3, 128, 4)
+
     result = on_chip(
-        join_rows, jax.ShapeDtypeStruct((4, 4, 32, 128), BF16), [smem, VMEM, VMEM],
-        place, out_ring, lax.ppermute(sent, "c", swap),
+        join_rows, jax.ShapeDtypeStruct((4, 4, 32, 128), BF16), [smem, VMEM, HBM], place, out_ring, piece,
         out_specs=HBM,
         scratch_shapes=[pltpu.VMEM((4, 4, 32, 128), BF16), pltpu.SemaphoreType.DMA],
         name="join_rows",

time: 122 us -> 122 us (level)
  the two profiles are of different devices: /device:TPU:1 before, /device:TPU:2 now
where the time goes in v5:
time: 122 us; the launch traced here: 121 us
  blocking collectives  48 us (39%)
  starting transfers between devices  41.3 us (34%)
  Pallas kernels  15.8 us (13%)
  waiting for transfers between devices  14.4 us (12%)
    all_to_all x5, starting transfers between devices, exchange(): return lax.all_to_all(array, axis, split_axis=0, concat_axis=0, tiled=True)  37 us
    all_gather x1, blocking collectives, on_device(): mine_taps = lax.all_gather(line[None], 'x', axis=0, tiled=True)  18.6 us
    all_gather x1, blocking collectives, on_device(): lax.all_gather(tiles.reshape(1, 4, 4, 2, 16, 128), 'zl', axis=0, tiled=True)  16.5 us
    pallas_call x9, Pallas kernels, on_chip(): pl.pallas_call(kernel, out_shape=shapes, in_specs=specs, out_specs=out_sp...  15.8 us
    all_to_all x5, waiting for transfers between devices, exchange(): return lax.all_to_all(array, axis, split_axis=0, concat_axis=0, tiled=True)  13.7 us
    all_gather x1, blocking collectives, on_device(): out_ring = lax.all_gather(out_line[None], 'x', axis=0, tiled=True)  12.8 us
  transfers between devices with their start and end apart: 7, of which 4 were waited for; matrix products, arithmetic and copies ran while one was open for 0% of the time, Pallas kernels for 3%

profile of v5, /device:TPU:2, one launch (start us, length us, event | category | flops | bytes accessed | tf_op | source)
XLA Modules:
  0.0 121.0 jit_solution(7658024303198029809)
XLA Ops:
  0.6 1.8 %pack_taps.1 = bf16[4,14,16,128]{3,2,1,0:T(8,128)(2,1)} custom-call(bf16[27,4,128]{2,1,0:T(4,128)(2,1)} %bitcast.35, bf16[27,4,128]{2,1,0:T(4,128)(2,1)} %bitcast.36), custom_call_target="tpu_custom_call" | custom-call | tf_op jit(solution)/shard_map/pack_taps/pallas_call | solution.py:306
  2.4 0.0 copy-start
  2.4 0.0 copy-start.1
  2.4 6.0 %all-to-all-start = ((bf16[4,14,16,128]{3,2,1,0:T(8,128)(2,1)}), bf16[4,14,16,128]{3,2,1,0:T(8,128)(2,1)S(1)}, u32[]{:S(2)}, u32[]{:S(2)}) async-start(bf16[4,14,16,128]{3,2,1,0:T(8,128)(2,1)} %pack_taps.1), calls=%async_computation | async-start | bytes 458752 | tf_op jit(solution)/shard_map/all_to_all | solution.py:321
  8.5 0.0 copy-done
  8.5 0.0 copy-done.1
  8.5 1.2 pack_rows.1.packed
  9.7 7.0 %all-to-all-done.after = bf16[4,14,16,128]{3,2,1,0:T(8,128)(2,1)S(1)} async-done(((bf16[4,14,16,128]{3,2,1,0:T(8,128)(2,1)}), bf16[4,14,16,128]{3,2,1,0:T(8,128)(2,1)S(1)}, u32[]{:S(2)}, u32[]{:S(2)}) %all-to-all-start) | async-done | bytes 229408 | tf_op jit(solution)/shard_map/all_to_all | solution.py:321
  16.7 5.7 %all-to-all-start.1 = ((bf16[16,12,16,128]{3,2,1,0:T(8,128)(2,1)}), bf16[16,12,16,128]{3,2,1,0:T(8,128)(2,1)S(1)}, u32[]{:S(2)}, u32[]{:S(2)}) async-start(bf16[16,12,16,128]{3,2,1,0:T(8,128)(2,1)} %hold.1), calls=%async_computation.1 | async-start | bytes 1572864 | tf_op jit(solution)/shard_map/all_to_all | solution.py:321
  22.4 18.6 %all-gather = bf16[16,14,16,128]{3,2,1,0:T(8,128)(2,1)S(1)} all-gather(bf16[4,14,16,128]{3,2,1,0:T(8,128)(2,1)S(1)} %all-to-all-done.after), channel_id=2, replica_groups=mesh['zl'=4,'x'=4,'c'=2,'zh'=4,'y'=4] {'x'}, dimensions={0}, use_global_device_ids=true | all-gather | bytes 1146880 | tf_op jit(solution)/shard_map/all_gather | solution.py:346
  41.0 1.9 %collective-permute-start.1 = (bf16[4,4,14,16,128]{4,3,2,1,0:T(8,128)(2,1)S(1)}, bf16[4,4,14,16,128]{4,3,2,1,0:T(8,128)(2,1)S(1)}, u32[]{:S(2)}, u32[]{:S(2)}) collective-permute-start(bf16[4,4,14,16,128]{4,3,2,1,0:T(8,128)(2,1)S(1)} %bitcast.25), channel_id=1, source_target_pairs={{0,16},{16,0},{1,17},{17,1},{2,18},{18,2},{3,19},{19,3},{4,20},{20... | collective-permute-start | bytes 2752520 | tf_op jit(solution)/shard_map/ppermute | solution.py:348
  42.9 0.0 all-to-all-done.1.mine
  42.9 2.4 %collective-permute-start = (bf16[16,12,16,128]{3,2,1,0:T(8,128)(2,1)S(1)}, bf16[16,12,16,128]{3,2,1,0:T(8,128)(2,1)S(1)}, u32[]{:S(2)}, u32[]{:S(2)}) collective-permute-start(bf16[16,12,16,128]{3,2,1,0:T(8,128)(2,1)S(1)} %all-to-all-done.1.mine), channel_id=1, source_target_pairs={{0,16},{16,0},{1,17},{17,1},{2,18},{18,2},{3,19},{19,3},{4,20},{20... | collective-permute-start | bytes 2359304 | tf_op jit(solution)/shard_map/ppermute | solution.py:348
  45.4 0.1 pad_add_fusion.place
  45.4 1.0 place_mine.1
  46.5 0.0 collective-permute-done.1.other_taps
  46.5 0.8 collective-permute-done.far
  47.3 8.4 %convolutions.1 = (bf16[16,2,16,128]{3,2,1,0:T(8,128)(2,1)S(1)}, bf16[4,4,14,16,128]{4,3,2,1,0:T(8,128)(2,1)}, bf16[512,1024]{1,0:T(8,128)(2,1)S(1)}, bf16[512,5...) custom-call(s32[2]{0:T(128)S(1)} %pad_add_fusion.place, ...), custom_call_target="tpu_custom_call", output_to_operand_aliasing={{2}: (3, {}), {3}: (4, {}), {4}: (5, {}), {5}: (6, {})} | custom-call | flops 6300000256 | bytes 6000000 | tf_op jit(solution)/shard_map/convolutions/pallas_call | solution.py:306
  55.7 7.2 %all-to-all-start.2 = ((bf16[16,14,16,128]{3,2,1,0:T(8,128)(2,1)}), bf16[16,14,16,128]{3,2,1,0:T(8,128)(2,1)S(1)}, u32[]{:S(2)}, u32[]{:S(2)}) async-start(bf16[16,14,16,128]{3,2,1,0:T(8,128)(2,1)} %bitcast.10), calls=%async_computation.2 | async-start | bytes 1835008 | tf_op jit(solution)/shard_map/all_to_all | solution.py:321
  62.8 16.5 %all_gather.10.after.line = bf16[4,4,4,2,16,128]{5,4,3,2,1,0:T(8,128)(2,1)S(1)} all-gather(bf16[1,4,4,2,16,128]{5,4,3,2,1,0:T(8,128)(2,1)S(1)} %bitcast.27), channel_id=1, replica_groups=mesh['zl'=4,'x'=4,'c'=2,'zh'=4,'y'=4] {'zl'}, dimensions={0}, use_global_device_ids=true | all-gather | bytes 655360 | tf_op jit(solution)/shard_map/all_gather | solution.py:353
  79.4 0.0 all-to-all-done.2.parts
  79.4 0.8 sum_ring.1.after
  80.2 13.8 %all-to-all-start.3 = ((bf16[16,56,128]{2,1,0:T(8,128)(2,1)}), bf16[16,56,128]{2,1,0:T(8,128)(2,1)S(1)}, u32[]{:S(2)}, u32[]{:S(2)}) async-start(bf16[16,56,128]{2,1,0:T(8,128)(2,1)} %sum_ring.1.after), calls=%async_computation.3 | async-start | bytes 458752 | tf_op jit(solution)/shard_map/all_to_all | solution.py:321
  94.0 0.6 pick_line.1
  94.6 12.8 %all-gather.1 = bf16[16,4,2,16,128]{4,3,2,1,0:T(8,128)(2,1)S(1)} all-gather(bf16[4,4,2,16,128]{4,3,2,1,0:T(8,128)(2,1)S(1)} %pick_line.1), channel_id=3, replica_groups=mesh['zl'=4,'x'=4,'c'=2,'zh'=4,'y'=4] {'x'}, dimensions={0}, use_global_device_ids=true | all-gather | bytes 655360 | tf_op jit(solution)/shard_map/all_gather | solution.py:363
  107.4 2.3 %all-to-all-done.3.pieces = bf16[16,56,128]{2,1,0:T(8,128)(2,1)S(1)} async-done(((bf16[16,56,128]{2,1,0:T(8,128)(2,1)}), bf16[16,56,128]{2,1,0:T(8,128)(2,1)S(1)}, u32[]{:S(2)}, u32[]{:S(2)}) %all-to-all-start.3) | async-done | bytes 229408 | tf_op jit(solution)/shard_map/all_to_all | solution.py:321
  109.7 0.8 sum_pieces.1.after
  110.5 4.2 %all-to-all-start.4 = ((bf16[4,56,128]{2,1,0:T(8,128)(2,1)}), bf16[4,56,128]{2,1,0:T(8,128)(2,1)S(1)}, u32[]{:S(2)}, u32[]{:S(2)}) async-start(bf16[4,56,128]{2,1,0:T(8,128)(2,1)} %sum_pieces.1.after), calls=%async_computation.4 | async-start | bytes 114688 | tf_op jit(solution)/shard_map/all_to_all | solution.py:321
  114.7 1.3 %join_rows.1 = bf16[4,4,32,128]{3,2,1,0:T(8,128)(2,1)} custom-call(s32[2]{0:T(128)S(1)} %pad_add_fusion.place, bf16[4,4,4,2,16,128]{5,4,3,2,1,0:T(8,128)(2,1)S(1)} %bitcast.24, bf16[4,56,128]{2,1,0:T(8,128)(2,1)} %sum_pieces.1.after), custom_call_target="tpu_custom_call" | custom-call | tf_op jit(solution)/shard_map/join_rows/pallas_call | solution.py:306
  116.0 4.3 %all-to-all-done.4 = bf16[4,56,128]{2,1,0:T(8,128)(2,1)S(1)} async-done(((bf16[4,56,128]{2,1,0:T(8,128)(2,1)}), bf16[4,56,128]{2,1,0:T(8,128)(2,1)S(1)}, u32[]{:S(2)}, u32[]{:S(2)}) %all-to-all-start.4) | async-done | bytes 57376 | tf_op jit(solution)/shard_map/all_to_all | solution.py:321
  120.4 0.6 fusion
  (3 shorter events, 0.0 us)
Async XLA Ops:
  2.4 6.1 %copy-start = (bf16[1,4,4,32,128]{4,3,2,1,0:T(8,128)(2,1)S(1)}, bf16[1,4,4,32,128]{4,3,2,1,0:T(8,128)(2,1)}, u32[]{:S(2)}) copy-start(bf16[1,4,4,32,128]{4,3,2,1,0:T(8,128)(2,1)} %param.4) | copy-start | bytes 393220
  2.4 6.1 %copy-start.1 = (bf16[1,4,4,32,128]{4,3,2,1,0:T(8,128)(2,1)S(1)}, bf16[1,4,4,32,128]{4,3,2,1,0:T(8,128)(2,1)}, u32[]{:S(2)}) copy-start(bf16[1,4,4,32,128]{4,3,2,1,0:T(8,128)(2,1)} %param.7) | copy-start | bytes 393220
  2.4 14.3 %all-to-all-start = ((bf16[4,14,16,128]{3,2,1,0:T(8,128)(2,1)}), bf16[4,14,16,128]{3,2,1,0:T(8,128)(2,1)S(1)}, u32[]{:S(2)}, u32[]{:S(2)}) async-start(bf16[4,14,16,128]{3,2,1,0:T(8,128)(2,1)} %pack_taps.1), calls=%async_computation | async-start | bytes 458752 | tf_op jit(solution)/shard_map/all_to_all | solution.py:321
  16.7 26.2 %all-to-all-start.1 = ((bf16[16,12,16,128]{3,2,1,0:T(8,128)(2,1)}), bf16[16,12,16,128]{3,2,1,0:T(8,128)(2,1)S(1)}, u32[]{:S(2)}, u32[]{:S(2)}) async-start(bf16[16,12,16,128]{3,2,1,0:T(8,128)(2,1)} %hold.1), calls=%async_computation.1 | async-start | bytes 1572864 | tf_op jit(solution)/shard_map/all_to_all | solution.py:321
  41.0 5.5 %collective-permute-start.1 = (bf16[4,4,14,16,128]{4,3,2,1,0:T(8,128)(2,1)S(1)}, bf16[4,4,14,16,128]{4,3,2,1,0:T(8,128)(2,1)S(1)}, u32[]{:S(2)}, u32[]{:S(2)}) collective-permute-start(bf16[4,4,14,16,128]{4,3,2,1,0:T(8,128)(2,1)S(1)} %bitcast.25), channel_id=1, source_target_pairs={{0,16},{16,0},{1,17},{17,1},{2,18},{18,2},{3,19},{19,3},{4,20},{20... | collective-permute-start | bytes 2752520 | tf_op jit(solution)/shard_map/ppermute | solution.py:348
  42.9 4.3 %collective-permute-start = (bf16[16,12,16,128]{3,2,1,0:T(8,128)(2,1)S(1)}, bf16[16,12,16,128]{3,2,1,0:T(8,128)(2,1)S(1)}, u32[]{:S(2)}, u32[]{:S(2)}) collective-permute-start(bf16[16,12,16,128]{3,2,1,0:T(8,128)(2,1)S(1)} %all-to-all-done.1.mine), channel_id=1, source_target_pairs={{0,16},{16,0},{1,17},{17,1},{2,18},{18,2},{3,19},{19,3},{4,20},{20... | collective-permute-start | bytes 2359304 | tf_op jit(solution)/shard_map/ppermute | solution.py:348
  55.7 23.7 %all-to-all-start.2 = ((bf16[16,14,16,128]{3,2,1,0:T(8,128)(2,1)}), bf16[16,14,16,128]{3,2,1,0:T(8,128)(2,1)S(1)}, u32[]{:S(2)}, u32[]{:S(2)}) async-start(bf16[16,14,16,128]{3,2,1,0:T(8,128)(2,1)} %bitcast.10), calls=%async_computation.2 | async-start | bytes 1835008 | tf_op jit(solution)/shard_map/all_to_all | solution.py:321
  80.2 29.5 %all-to-all-start.3 = ((bf16[16,56,128]{2,1,0:T(8,128)(2,1)}), bf16[16,56,128]{2,1,0:T(8,128)(2,1)S(1)}, u32[]{:S(2)}, u32[]{:S(2)}) async-start(bf16[16,56,128]{2,1,0:T(8,128)(2,1)} %sum_ring.1.after), calls=%async_computation.3 | async-start | bytes 458752 | tf_op jit(solution)/shard_map/all_to_all | solution.py:321
  110.5 9.8 %all-to-all-start.4 = ((bf16[4,56,128]{2,1,0:T(8,128)(2,1)}), bf16[4,56,128]{2,1,0:T(8,128)(2,1)S(1)}, u32[]{:S(2)}, u32[]{:S(2)}) async-start(bf16[4,56,128]{2,1,0:T(8,128)(2,1)} %sum_pieces.1.after), calls=%async_computation.4 | async-start | bytes 114688 | tf_op jit(solution)/shard_map/all_to_all | solution.py:321

commit v6 on v5

--- a/solution.py
+++ b/solution.py
@@ -257,7 +257,7 @@
     pass
 
 
-def sum_ring(parts, after, out):
+def sum_ring(parts, one, two, three, out):
     total = parts[0].astype(F32)
     for n in range(1, 16):
         total = total + parts[n].astype(F32)
@@ -278,9 +278,14 @@
         total[y] = found
 
 
-def pick_line(place, line, after, out):
-    for zl in range(4):
-        out[zl] = line[zl, place[1] // 4]
+def pick_line(place, tiles, *outs):
+    for m, out in enumerate(outs):
+        out[...] = tiles[pl.ds((place[1] // 4 ^ m) * 4, 4)]
+
+
+def join_line(own, one, two, three, after, out):
+    for m, tiles in enumerate((own, one, two, three)):
+        out[m] = tiles[...]
 
 
 def join_rows(place, ring, after, out, near, sent):
@@ -288,7 +293,7 @@
     for zl in range(4):
         for x in range(4):
             for r in range(2):
-                tiles.append(ring[x, zl, place[1] % 4, r].astype(F32))
+                tiles.append(ring[x, zl ^ (place[1] // 4), place[1] % 4, r].astype(F32))
     rows = jnp.swapaxes(jnp.stack(tiles), 0, 1).astype(BF16)
     for z in range(4):
         for ch in range(4):
@@ -350,15 +355,19 @@
     tiles, grads = compute(place, mine, other, mine_taps, other_taps)
 
     parts = exchange(grads.reshape(16, 14, 16, 128), ("x", "y"))
-    out_line = lax.all_gather(tiles.reshape(1, 4, 4, 2, 16, 128), "zl", axis=0, tiled=True)
+    smem = pl.BlockSpec(memory_space=pltpu.SMEM)
+    tile = jax.ShapeDtypeStruct((4, 2, 16, 128), BF16)
+    own, *sent = on_chip(pick_line, (tile,) * 4, [smem, VMEM], place, tiles, out_specs=(VMEM,) * 4, name="pick_line")
+    came = [
+        lax.ppermute(part, "zl", [(i, i ^ m) for i in range(4)]) for m, part in zip((1, 2, 3), sent)
+    ]
     spread = on_chip(
-        sum_ring, jax.ShapeDtypeStruct((16, 56, 128), BF16), [VMEM, HBM], parts, out_line, name="sum_ring"
+        sum_ring, jax.ShapeDtypeStruct((16, 56, 128), BF16), [VMEM, HBM, HBM, HBM], parts, *came, name="sum_ring"
     )
     depth = exchange(spread, ("zh", "zl"))
-    smem = pl.BlockSpec(memory_space=pltpu.SMEM)
     out_line = on_chip(
-        pick_line, jax.ShapeDtypeStruct((4, 4, 2, 16, 128), BF16), [smem, VMEM, HBM],
-        place, out_line, spread, name="pick_line",
+        join_line, jax.ShapeDtypeStruct((4, 4, 2, 16, 128), BF16), [VMEM] * 4 + [HBM],
+        own, *came, spread, name="join_line",
     )
     out_ring = lax.all_gather(out_line[None], "x", axis=0, tiled=True)
     piece = on_chip(

time: 122 us -> 122 us (level)
  blocking collectives: 48 us -> 31.4 us
  starting transfers between devices: 41.3 us -> 51 us
  waiting for transfers between devices: 14.4 us -> 21.1 us
    all_gather x1 -> x0, blocking collectives: 16.5 us -> none  [on_device(): lax.all_gather(tiles.reshape(1, 4, 4, 2, 16, 128), 'zl', axis=0, tiled=True)]
    ppermute x0 -> x3, starting transfers between devices: none -> 10.5 us  [on_device(): lax.ppermute(part, 'zl', [(i, i ^ m) for i in range(4)])]
    ppermute x0 -> x3, waiting for transfers between devices: none -> 5.66 us  [on_device(): lax.ppermute(part, 'zl', [(i, i ^ m) for i in range(4)])]
    pallas_call x9 -> x10, Pallas kernels: 15.8 us -> 15.8 us  [on_chip(): pl.pallas_call(kernel, out_shape=shapes, in_specs=specs, out_specs=out_sp...]
  transfers between devices with their start and end apart: 7 -> 10, of which waited for: 4 -> 5; matrix products, arithmetic and copies ran while one was open for 0% -> 0% of each run, Pallas kernels for 3% -> 3%
where the time goes in v6:
time: 122 us; the launch traced here: 121 us
  starting transfers between devices  51 us (42%)
  blocking collectives  31.4 us (26%)
  waiting for transfers between devices  21.1 us (17%)
  Pallas kernels  15.8 us (13%)
    all_to_all x5, starting transfers between devices, exchange(): return lax.all_to_all(array, axis, split_axis=0, concat_axis=0, tiled=True)  36.1 us
    all_gather x1, blocking collectives, on_device(): mine_taps = lax.all_gather(line[None], 'x', axis=0, tiled=True)  18.6 us
    pallas_call x10, Pallas kernels, on_chip(): pl.pallas_call(kernel, out_shape=shapes, in_specs=specs, out_specs=out_sp...  15.8 us
    all_to_all x5, waiting for transfers between devices, exchange(): return lax.all_to_all(array, axis, split_axis=0, concat_axis=0, tiled=True)  14.6 us
    all_gather x1, blocking collectives, on_device(): out_ring = lax.all_gather(out_line[None], 'x', axis=0, tiled=True)  12.8 us
    ppermute x3, starting transfers between devices, on_device(): lax.ppermute(part, 'zl', [(i, i ^ m) for i in range(4)])  10.5 us
    ppermute x3, waiting for transfers between devices, on_device(): lax.ppermute(part, 'zl', [(i, i ^ m) for i in range(4)])  5.66 us
  transfers between devices with their start and end apart: 10, of which 5 were waited for; matrix products, arithmetic and copies ran while one was open for 0% of the time, Pallas kernels for 3%

profile of v6, /device:TPU:2, one launch (start us, length us, event | category | flops | bytes accessed | tf_op | source)
XLA Modules:
  0.0 120.8 jit_solution(1405679139260782839)
XLA Ops:
  0.6 1.8 %pack_taps.1 = bf16[4,14,16,128]{3,2,1,0:T(8,128)(2,1)} custom-call(bf16[27,4,128]{2,1,0:T(4,128)(2,1)} %bitcast.33, bf16[27,4,128]{2,1,0:T(4,128)(2,1)} %bitcast.34), custom_call_target="tpu_custom_call" | custom-call | tf_op jit(solution)/shard_map/pack_taps/pallas_call | solution.py:311
  2.4 0.0 copy-start
  2.4 0.0 copy-start.1
  2.4 6.0 %all-to-all-start = ((bf16[4,14,16,128]{3,2,1,0:T(8,128)(2,1)}), bf16[4,14,16,128]{3,2,1,0:T(8,128)(2,1)S(1)}, u32[]{:S(2)}, u32[]{:S(2)}) async-start(bf16[4,14,16,128]{3,2,1,0:T(8,128)(2,1)} %pack_taps.1), calls=%async_computation | async-start | bytes 458752 | tf_op jit(solution)/shard_map/all_to_all | solution.py:326
  8.5 0.0 copy-done
  8.5 0.0 copy-done.1
  8.5 1.1 pack_rows.1.packed
  9.6 7.1 %all-to-all-done.after = bf16[4,14,16,128]{3,2,1,0:T(8,128)(2,1)S(1)} async-done(((bf16[4,14,16,128]{3,2,1,0:T(8,128)(2,1)}), bf16[4,14,16,128]{3,2,1,0:T(8,128)(2,1)S(1)}, u32[]{:S(2)}, u32[]{:S(2)}) %all-to-all-start) | async-done | bytes 229408 | tf_op jit(solution)/shard_map/all_to_all | solution.py:326
  16.7 5.7 %all-to-all-start.1 = ((bf16[16,12,16,128]{3,2,1,0:T(8,128)(2,1)}), bf16[16,12,16,128]{3,2,1,0:T(8,128)(2,1)S(1)}, u32[]{:S(2)}, u32[]{:S(2)}) async-start(bf16[16,12,16,128]{3,2,1,0:T(8,128)(2,1)} %hold.1), calls=%async_computation.1 | async-start | bytes 1572864 | tf_op jit(solution)/shard_map/all_to_all | solution.py:326
  22.4 18.6 %all-gather = bf16[16,14,16,128]{3,2,1,0:T(8,128)(2,1)S(1)} all-gather(bf16[4,14,16,128]{3,2,1,0:T(8,128)(2,1)S(1)} %all-to-all-done.after), channel_id=2, replica_groups=mesh['zl'=4,'x'=4,'c'=2,'zh'=4,'y'=4] {'x'}, dimensions={0}, use_global_device_ids=true | all-gather | bytes 1146880 | tf_op jit(solution)/shard_map/all_gather | solution.py:351
  41.0 1.9 %collective-permute-start.1 = (bf16[4,4,14,16,128]{4,3,2,1,0:T(8,128)(2,1)S(1)}, bf16[4,4,14,16,128]{4,3,2,1,0:T(8,128)(2,1)S(1)}, u32[]{:S(2)}, u32[]{:S(2)}) collective-permute-start(bf16[4,4,14,16,128]{4,3,2,1,0:T(8,128)(2,1)S(1)} %bitcast.24), channel_id=1, source_target_pairs={{0,16},{16,0},{1,17},{17,1},{2,18},{18,2},{3,19},{19,3},{4,20},{20... | collective-permute-start | bytes 2752520 | tf_op jit(solution)/shard_map/ppermute | solution.py:353
  42.9 0.0 all-to-all-done.1.mine
  42.9 2.4 %collective-permute-start = (bf16[16,12,16,128]{3,2,1,0:T(8,128)(2,1)S(1)}, bf16[16,12,16,128]{3,2,1,0:T(8,128)(2,1)S(1)}, u32[]{:S(2)}, u32[]{:S(2)}) collective-permute-start(bf16[16,12,16,128]{3,2,1,0:T(8,128)(2,1)S(1)} %all-to-all-done.1.mine), channel_id=1, source_target_pairs={{0,16},{16,0},{1,17},{17,1},{2,18},{18,2},{3,19},{19,3},{4,20},{20... | collective-permute-start | bytes 2359304 | tf_op jit(solution)/shard_map/ppermute | solution.py:353
  45.4 0.1 pad_add_fusion.place
  45.4 1.0 place_mine.1
  46.5 0.0 collective-permute-done.1.other_taps
  46.5 0.8 collective-permute-done.far
  47.2 8.4 %convolutions.1 = (bf16[16,2,16,128]{3,2,1,0:T(8,128)(2,1)S(1)}, bf16[4,4,14,16,128]{4,3,2,1,0:T(8,128)(2,1)}, bf16[512,1024]{1,0:T(8,128)(2,1)S(1)}, bf16[512,5...) custom-call(s32[2]{0:T(128)S(1)} %pad_add_fusion.place, ...), custom_call_target="tpu_custom_call", output_to_operand_aliasing={{2}: (3, {}), {3}: (4, {}), {4}: (5, {}), {5}: (6, {})} | custom-call | flops 6300000256 | bytes 6000000 | tf_op jit(solution)/shard_map/convolutions/pallas_call | solution.py:311
  55.7 7.2 %all-to-all-start.2 = ((bf16[16,14,16,128]{3,2,1,0:T(8,128)(2,1)}), bf16[16,14,16,128]{3,2,1,0:T(8,128)(2,1)S(1)}, u32[]{:S(2)}, u32[]{:S(2)}) async-start(bf16[16,14,16,128]{3,2,1,0:T(8,128)(2,1)} %bitcast.9), calls=%async_computation.2 | async-start | bytes 1835008 | tf_op jit(solution)/shard_map/all_to_all | solution.py:326
  62.8 0.6 pick_line.1
  63.4 3.1 %collective-permute-start.2 = (bf16[4,2,16,128]{3,2,1,0:T(8,128)(2,1)S(1)}, bf16[4,2,16,128]{3,2,1,0:T(8,128)(2,1)S(1)}, u32[]{:S(2)}, u32[]{:S(2)}) collective-permute-start(bf16[4,2,16,128]{3,2,1,0:T(8,128)(2,1)S(1)} %get-tuple-element.19), channel_id=1, source_target_pairs={{0,128},{128,0},{256,384},{384,256},{1,129},{129,1},{257,385},{385... | collective-permute-start | bytes 98312 | tf_op jit(solution)/shard_map/ppermute | solution.py:362
  66.5 5.5 %collective-permute-start.3 = (bf16[4,2,16,128]{3,2,1,0:T(8,128)(2,1)S(1)}, bf16[4,2,16,128]{3,2,1,0:T(8,128)(2,1)S(1)}, u32[]{:S(2)}, u32[]{:S(2)}) collective-permute-start(bf16[4,2,16,128]{3,2,1,0:T(8,128)(2,1)S(1)} %get-tuple-element.20), channel_id=1, source_target_pairs={{0,256},{128,384},{256,0},{384,128},{1,257},{129,385},{257,1},{385... | collective-permute-start | bytes 98312 | tf_op jit(solution)/shard_map/ppermute | solution.py:362
  72.0 1.9 %collective-permute-start.4 = (bf16[4,2,16,128]{3,2,1,0:T(8,128)(2,1)S(1)}, bf16[4,2,16,128]{3,2,1,0:T(8,128)(2,1)S(1)}, u32[]{:S(2)}, u32[]{:S(2)}) collective-permute-start(bf16[4,2,16,128]{3,2,1,0:T(8,128)(2,1)S(1)} %get-tuple-element.21), channel_id=1, source_target_pairs={{0,384},{128,256},{256,128},{384,0},{1,385},{129,257},{257,129},{3... | collective-permute-start | bytes 98312 | tf_op jit(solution)/shard_map/ppermute | solution.py:362
  74.0 0.0 collective-permute-done.2.one
  74.0 0.0 collective-permute-done.3.two
  74.0 5.7 %collective-permute-done.4.three = bf16[4,2,16,128]{3,2,1,0:T(8,128)(2,1)S(1)} collective-permute-done((bf16[4,2,16,128]{3,2,1,0:T(8,128)(2,1)S(1)}, bf16[4,2,16,128]{3,2,1,0:T(8,128)(2,1)S(1)}, u32[]{:S(2)}, u32[]{:S(2)}) %collective-permute-start.4) | collective-permute-done | bytes 32800 | tf_op jit(solution)/shard_map/ppermute | solution.py:362
  79.7 0.0 all-to-all-done.2.parts
  79.7 0.8 sum_ring.1.after
  80.5 12.9 %all-to-all-start.3 = ((bf16[16,56,128]{2,1,0:T(8,128)(2,1)}), bf16[16,56,128]{2,1,0:T(8,128)(2,1)S(1)}, u32[]{:S(2)}, u32[]{:S(2)}) async-start(bf16[16,56,128]{2,1,0:T(8,128)(2,1)} %sum_ring.1.after), calls=%async_computation.3 | async-start | bytes 458752 | tf_op jit(solution)/shard_map/all_to_all | solution.py:326
  93.4 12.8 %all-gather.1 = bf16[16,4,2,16,128]{4,3,2,1,0:T(8,128)(2,1)S(1)} all-gather(bf16[4,4,2,16,128]{4,3,2,1,0:T(8,128)(2,1)S(1)} %join_line.1), channel_id=3, replica_groups=mesh['zl'=4,'x'=4,'c'=2,'zh'=4,'y'=4] {'x'}, dimensions={0}, use_global_device_ids=true | all-gather | bytes 655360 | tf_op jit(solution)/shard_map/all_gather | solution.py:372
  106.2 3.3 %all-to-all-done.3.pieces = bf16[16,56,128]{2,1,0:T(8,128)(2,1)S(1)} async-done(((bf16[16,56,128]{2,1,0:T(8,128)(2,1)}), bf16[16,56,128]{2,1,0:T(8,128)(2,1)S(1)}, u32[]{:S(2)}, u32[]{:S(2)}) %all-to-all-start.3) | async-done | bytes 229408 | tf_op jit(solution)/shard_map/all_to_all | solution.py:326
  109.5 0.8 sum_pieces.1.after
  110.3 4.2 %all-to-all-start.4 = ((bf16[4,56,128]{2,1,0:T(8,128)(2,1)}), bf16[4,56,128]{2,1,0:T(8,128)(2,1)S(1)}, u32[]{:S(2)}, u32[]{:S(2)}) async-start(bf16[4,56,128]{2,1,0:T(8,128)(2,1)} %sum_pieces.1.after), calls=%async_computation.4 | async-start | bytes 114688 | tf_op jit(solution)/shard_map/all_to_all | solution.py:326
  114.5 1.3 %join_rows.1 = bf16[4,4,32,128]{3,2,1,0:T(8,128)(2,1)} custom-call(s32[2]{0:T(128)S(1)} %pad_add_fusion.place, bf16[4,4,4,2,16,128]{5,4,3,2,1,0:T(8,128)(2,1)S(1)} %bitcast.23, bf16[4,56,128]{2,1,0:T(8,128)(2,1)} %sum_pieces.1.after), custom_call_target="tpu_custom_call" | custom-call | tf_op jit(solution)/shard_map/join_rows/pallas_call | solution.py:311
  115.8 4.3 %all-to-all-done.4 = bf16[4,56,128]{2,1,0:T(8,128)(2,1)S(1)} async-done(((bf16[4,56,128]{2,1,0:T(8,128)(2,1)}), bf16[4,56,128]{2,1,0:T(8,128)(2,1)S(1)}, u32[]{:S(2)}, u32[]{:S(2)}) %all-to-all-start.4) | async-done | bytes 57376 | tf_op jit(solution)/shard_map/all_to_all | solution.py:326
  120.2 0.6 fusion
  (4 shorter events, 0.0 us)
Async XLA Ops:
  2.4 6.1 %copy-start = (bf16[1,4,4,32,128]{4,3,2,1,0:T(8,128)(2,1)S(1)}, bf16[1,4,4,32,128]{4,3,2,1,0:T(8,128)(2,1)}, u32[]{:S(2)}) copy-start(bf16[1,4,4,32,128]{4,3,2,1,0:T(8,128)(2,1)} %param.4) | copy-start | bytes 393220
  2.4 6.1 %copy-start.1 = (bf16[1,4,4,32,128]{4,3,2,1,0:T(8,128)(2,1)S(1)}, bf16[1,4,4,32,128]{4,3,2,1,0:T(8,128)(2,1)}, u32[]{:S(2)}) copy-start(bf16[1,4,4,32,128]{4,3,2,1,0:T(8,128)(2,1)} %param.7) | copy-start | bytes 393220
  2.4 14.3 %all-to-all-start = ((bf16[4,14,16,128]{3,2,1,0:T(8,128)(2,1)}), bf16[4,14,16,128]{3,2,1,0:T(8,128)(2,1)S(1)}, u32[]{:S(2)}, u32[]{:S(2)}) async-start(bf16[4,14,16,128]{3,2,1,0:T(8,128)(2,1)} %pack_taps.1), calls=%async_computation | async-start | bytes 458752 | tf_op jit(solution)/shard_map/all_to_all | solution.py:326
  16.7 26.2 %all-to-all-start.1 = ((bf16[16,12,16,128]{3,2,1,0:T(8,128)(2,1)}), bf16[16,12,16,128]{3,2,1,0:T(8,128)(2,1)S(1)}, u32[]{:S(2)}, u32[]{:S(2)}) async-start(bf16[16,12,16,128]{3,2,1,0:T(8,128)(2,1)} %hold.1), calls=%async_computation.1 | async-start | bytes 1572864 | tf_op jit(solution)/shard_map/all_to_all | solution.py:326
  41.0 5.5 %collective-permute-start.1 = (bf16[4,4,14,16,128]{4,3,2,1,0:T(8,128)(2,1)S(1)}, bf16[4,4,14,16,128]{4,3,2,1,0:T(8,128)(2,1)S(1)}, u32[]{:S(2)}, u32[]{:S(2)}) collective-permute-start(bf16[4,4,14,16,128]{4,3,2,1,0:T(8,128)(2,1)S(1)} %bitcast.24), channel_id=1, source_target_pairs={{0,16},{16,0},{1,17},{17,1},{2,18},{18,2},{3,19},{19,3},{4,20},{20... | collective-permute-start | bytes 2752520 | tf_op jit(solution)/shard_map/ppermute | solution.py:353
  42.9 4.3 %collective-permute-start = (bf16[16,12,16,128]{3,2,1,0:T(8,128)(2,1)S(1)}, bf16[16,12,16,128]{3,2,1,0:T(8,128)(2,1)S(1)}, u32[]{:S(2)}, u32[]{:S(2)}) collective-permute-start(bf16[16,12,16,128]{3,2,1,0:T(8,128)(2,1)S(1)} %all-to-all-done.1.mine), channel_id=1, source_target_pairs={{0,16},{16,0},{1,17},{17,1},{2,18},{18,2},{3,19},{19,3},{4,20},{20... | collective-permute-start | bytes 2359304 | tf_op jit(solution)/shard_map/ppermute | solution.py:353
  55.7 24.0 %all-to-all-start.2 = ((bf16[16,14,16,128]{3,2,1,0:T(8,128)(2,1)}), bf16[16,14,16,128]{3,2,1,0:T(8,128)(2,1)S(1)}, u32[]{:S(2)}, u32[]{:S(2)}) async-start(bf16[16,14,16,128]{3,2,1,0:T(8,128)(2,1)} %bitcast.9), calls=%async_computation.2 | async-start | bytes 1835008 | tf_op jit(solution)/shard_map/all_to_all | solution.py:326
  63.4 10.6 %collective-permute-start.2 = (bf16[4,2,16,128]{3,2,1,0:T(8,128)(2,1)S(1)}, bf16[4,2,16,128]{3,2,1,0:T(8,128)(2,1)S(1)}, u32[]{:S(2)}, u32[]{:S(2)}) collective-permute-start(bf16[4,2,16,128]{3,2,1,0:T(8,128)(2,1)S(1)} %get-tuple-element.19), channel_id=1, source_target_pairs={{0,128},{128,0},{256,384},{384,256},{1,129},{129,1},{257,385},{385... | collective-permute-start | bytes 98312 | tf_op jit(solution)/shard_map/ppermute | solution.py:362
  66.5 7.5 %collective-permute-start.3 = (bf16[4,2,16,128]{3,2,1,0:T(8,128)(2,1)S(1)}, bf16[4,2,16,128]{3,2,1,0:T(8,128)(2,1)S(1)}, u32[]{:S(2)}, u32[]{:S(2)}) collective-permute-start(bf16[4,2,16,128]{3,2,1,0:T(8,128)(2,1)S(1)} %get-tuple-element.20), channel_id=1, source_target_pairs={{0,256},{128,384},{256,0},{384,128},{1,257},{129,385},{257,1},{385... | collective-permute-start | bytes 98312 | tf_op jit(solution)/shard_map/ppermute | solution.py:362
  72.0 7.6 %collective-permute-start.4 = (bf16[4,2,16,128]{3,2,1,0:T(8,128)(2,1)S(1)}, bf16[4,2,16,128]{3,2,1,0:T(8,128)(2,1)S(1)}, u32[]{:S(2)}, u32[]{:S(2)}) collective-permute-start(bf16[4,2,16,128]{3,2,1,0:T(8,128)(2,1)S(1)} %get-tuple-element.21), channel_id=1, source_target_pairs={{0,384},{128,256},{256,128},{384,0},{1,385},{129,257},{257,129},{3... | collective-permute-start | bytes 98312 | tf_op jit(solution)/shard_map/ppermute | solution.py:362
  80.5 29.0 %all-to-all-start.3 = ((bf16[16,56,128]{2,1,0:T(8,128)(2,1)}), bf16[16,56,128]{2,1,0:T(8,128)(2,1)S(1)}, u32[]{:S(2)}, u32[]{:S(2)}) async-start(bf16[16,56,128]{2,1,0:T(8,128)(2,1)} %sum_ring.1.after), calls=%async_computation.3 | async-start | bytes 458752 | tf_op jit(solution)/shard_map/all_to_all | solution.py:326
  110.3 9.8 %all-to-all-start.4 = ((bf16[4,56,128]{2,1,0:T(8,128)(2,1)}), bf16[4,56,128]{2,1,0:T(8,128)(2,1)S(1)}, u32[]{:S(2)}, u32[]{:S(2)}) async-start(bf16[4,56,128]{2,1,0:T(8,128)(2,1)} %sum_pieces.1.after), calls=%async_computation.4 | async-start | bytes 114688 | tf_op jit(solution)/shard_map/all_to_all | solution.py:326
